TPU v7x, 256 devices: a whole 4x4x8 slice. The times are simulated.
256 devices in a mesh: group: 8 (over y, z_lo), dev: 32 (over z_hi, x, core).
Axes of the slice: x: 4, y: 4, z: 8 (z_hi: 4, z_lo: 2; z = z_hi * 2 + z_lo), core: 2. Of those that a mesh axis runs over, the one named last changes fastest.
Arguments:
- tokens: bfloat16 [4096, 2560], P(('group', 'dev')), may hold values from -6 to 6
- grad_out: bfloat16 [4096, 2560], P(('group', 'dev')), may hold values from -6 to 6
- routes: int32 [4096, 6], P(('group', 'dev')), may hold values from 0 to 23, all different within a row; in each aligned block of 16 rows (0 to 15, 16 to 31, ...) at most 6 rows name the same one
- gates: bfloat16 [4096, 6], P(('group', 'dev')), may hold values from 0.049804688 to 0.5
- pull_list: int32 [8, 8], replicated, may hold values from 0 to 127, as said below
- counts: int32 [8], replicated, may hold values from 1 to 512, 2304 in all
- w_gate: bfloat16 [256, 2560, 384], P(('group', 'dev')), may hold values from -0.125 to 0.125
- w_up: bfloat16 [256, 2560, 384], P(('group', 'dev')), may hold values from -0.125 to 0.125
- w_down: bfloat16 [256, 384, 2560], P(('group', 'dev')), may hold values from -0.21875 to 0.21875
Outputs:
- mixed: bfloat16 [4096, 2560], P(('group', 'dev'))
- token_grad: bfloat16 [4096, 2560], P(('group', 'dev'))
- grad_gate: bfloat16 [256, 2560, 384], P(('group', 'dev'))
- grad_up: bfloat16 [256, 2560, 384], P(('group', 'dev'))
- grad_down: bfloat16 [256, 384, 2560], P(('group', 'dev'))
Inputs may be any that keep to these rules, and one draw needn't show every extreme that they name: `routes`: the rows of one device name each slot at most 6 times, a bound that some block reaches. `pull_list`: row g holds 8 distinct experts of group (g - 1) mod 8; expert e belongs to group e // 16. `counts`: some group has all its rows live.
All inputs are finite; a program needn't handle non-finite values.
Results may differ from a plain program's by a relative error of at most 0.01.
Values may be sent and summed in bfloat16 or wider, within the bound.
A program may use at most 128 MiB of HBM per device.

v0:
```python
import jax
import jax.numpy as jnp
from jax import lax
from jax.sharding import PartitionSpec as P

SLICES = 2


def for_sending(x):
    return jax.tree.map(lambda a: a.astype(jnp.bfloat16) if a.dtype == jnp.float32 else a, x)


def passed_along(x, axis, by):
    length = lax.axis_size(axis)
    return lax.ppermute(x, axis, [(i, (i + by) % length) for i in range(length)])


def expert_pass(rows_x, rows_dy, rows_gate, weight_gate, weight_up, weight_down):
    pre_gate = jnp.dot(rows_x, weight_gate, preferred_element_type=jnp.float32)
    pre_up = jnp.dot(rows_x, weight_up, preferred_element_type=jnp.float32)
    sigmoid_gate = jax.nn.sigmoid(pre_gate)
    activated = pre_gate * sigmoid_gate
    gate_scale = rows_gate.astype(jnp.float32)[:, None]
    gated_hidden = (gate_scale * activated * pre_up).astype(jnp.bfloat16)
    partial_out = jnp.dot(gated_hidden, weight_down, preferred_element_type=jnp.float32).astype(
        jnp.bfloat16
    )
    back_hidden = jnp.dot(rows_dy, weight_down.T, preferred_element_type=jnp.float32) * gate_scale
    grad_pre_gate = (
        back_hidden * pre_up * sigmoid_gate * (1.0 + pre_gate * (1.0 - sigmoid_gate))
    ).astype(jnp.bfloat16)
    grad_pre_up = (back_hidden * activated).astype(jnp.bfloat16)
    partial_dx = (
        jnp.dot(grad_pre_gate, weight_gate.T, preferred_element_type=jnp.float32)
        + jnp.dot(grad_pre_up, weight_up.T, preferred_element_type=jnp.float32)
    ).astype(jnp.bfloat16)
    sum_gate = jnp.dot(rows_x.T, grad_pre_gate, preferred_element_type=jnp.float32).astype(
        jnp.bfloat16
    )
    sum_up = jnp.dot(rows_x.T, grad_pre_up, preferred_element_type=jnp.float32).astype(jnp.bfloat16)
    sum_down = jnp.dot(gated_hidden.T, rows_dy, preferred_element_type=jnp.float32).astype(
        jnp.bfloat16
    )
    return (partial_out, partial_dx, sum_gate, sum_up, sum_down)


def shards(tokens, grad_out, routes, gates, pull_list, counts, w_gate, w_up, w_down):
    dev_count = lax.axis_size("dev")
    tok_rows = tokens.shape[0]
    width = tokens.shape[1]
    top_count = routes.shape[1]
    pull_count = pull_list.shape[1]
    local_experts = dev_count // SLICES
    slot_count = local_experts + pull_count
    capacity = 3 * tok_rows * top_count // (2 * slot_count)
    group_id = lax.axis_index("group")
    dev_id = lax.axis_index("dev")
    alive = dev_id * tok_rows + jnp.arange(tok_rows) < counts[group_id]
    flat_slot = routes.reshape(-1)
    flat_live = jnp.repeat(alive, top_count)
    member = ((flat_slot[:, None] == jnp.arange(slot_count)[None, :]) & flat_live[:, None]).astype(
        jnp.int32
    )
    earlier = jnp.cumsum(member, axis=0) - member
    position = jnp.sum(earlier * member, axis=1)
    pair_ids = jnp.arange(tok_rows * top_count)
    placed = member[:, :, None] * (
        position[:, None, None] == jnp.arange(capacity)[None, None, :]
    ).astype(jnp.int32)
    source_pair = jnp.sum(placed * (pair_ids[:, None, None] + 1), axis=0) - 1
    target_local = jnp.arange(dev_count) // SLICES
    pull_row = pull_list[group_id]
    pull_match = pull_row[None, :] % local_experts == target_local[:, None]
    pull_slot = jnp.where(
        jnp.any(pull_match, axis=1),
        local_experts + jnp.sum(jnp.where(pull_match, jnp.arange(pull_count)[None, :], 0), axis=1),
        -1,
    )
    dest_slot = jnp.stack([target_local, pull_slot], axis=0)
    table = jnp.where(dest_slot[:, :, None] >= 0, source_pair[jnp.maximum(dest_slot, 0)], -1)
    flat_gates = gates.reshape(-1)
    present = table >= 0
    safe_index = jnp.maximum(table, 0)
    token_of = safe_index // top_count
    zero_value = jnp.zeros((), jnp.bfloat16)
    outgoing_input = jnp.where(present[..., None], tokens[token_of], zero_value)
    send_dy = jnp.where(present[..., None], grad_out[token_of], zero_value)
    send_gate = jnp.where(present, flat_gates[safe_index], zero_value)
    received = lax.all_to_all(
        for_sending((outgoing_input, send_dy, send_gate)),
        "dev",
        split_axis=1,
        concat_axis=1,
        tiled=True,
    )
    block_rows = dev_count * capacity
    recv_x = received[0].reshape(2, block_rows, width)
    recv_dy = received[1].reshape(2, block_rows, width)
    recv_gate = received[2].reshape(2, block_rows)
    owned = expert_pass(recv_x[0], recv_dy[0], recv_gate[0], w_gate[0], w_up[0], w_down[0])
    far_gate, far_up, far_down = passed_along((w_gate, w_up, w_down), "group", 1)
    borrowed = expert_pass(recv_x[1], recv_dy[1], recv_gate[1], far_gate[0], far_up[0], far_down[0])
    returned = passed_along((borrowed[2], borrowed[3], borrowed[4]), "group", -1)
    far_out = borrowed[0]
    far_dx = borrowed[1]
    weight_grads = tuple(
        (
            (own_part.astype(jnp.float32) + other_part.astype(jnp.float32)).astype(jnp.bfloat16)[
                None
            ]
            for own_part, other_part in zip(owned[2:], returned)
        )
    )
    back_out = jnp.stack([owned[0], far_out]).reshape(2, dev_count, capacity, width)
    back_dx = jnp.stack([owned[1], far_dx]).reshape(2, dev_count, capacity, width)
    got_out, got_dx = (
        lax.all_to_all(back_out, "dev", split_axis=1, concat_axis=1, tiled=True),
        lax.all_to_all(back_dx, "dev", split_axis=1, concat_axis=1, tiled=True),
    )
    token_of = jnp.where(table >= 0, table // top_count, -1).reshape(-1)
    selector = (token_of[None, :] == jnp.arange(tok_rows)[:, None]).astype(jnp.bfloat16)
    mixed = jnp.dot(
        selector, got_out.reshape(-1, width), preferred_element_type=jnp.float32
    ).astype(jnp.bfloat16)
    token_grad = jnp.dot(
        selector, got_dx.reshape(-1, width), preferred_element_type=jnp.float32
    ).astype(jnp.bfloat16)
    return (mixed, token_grad, weight_grads[0], weight_grads[1], weight_grads[2])


def solution(mesh):
    in_specs = (
        P(("group", "dev"), None),
        P(("group", "dev"), None),
        P(("group", "dev"), None),
        P(("group", "dev"), None),
        P(),
        P(),
        P(("group", "dev"), None, None),
        P(("group", "dev"), None, None),
        P(("group", "dev"), None, None),
    )
    out_specs = (
        P(("group", "dev"), None),
        P(("group", "dev"), None),
        P(("group", "dev"), None, None),
        P(("group", "dev"), None, None),
        P(("group", "dev"), None, None),
    )
    return jax.shard_map(shards, mesh=mesh, in_specs=in_specs, out_specs=out_specs, check_vma=False)
```

profile of v0, /device:TPU:1, one launch (start us, length us, event | category | flops | bytes accessed | tf_op | source)
XLA Modules:
  0.0 548.1 jit_solution(8308960097557188015)
XLA Ops:
  7.2 2.7 gather_fusion.1
  10.7 12.6 %all-to-all-start = ((bf16[2,32,6]{2,0,1:T(2,128)(2,1)}), bf16[2,32,6]{2,0,1:T(2,128)(2,1)S(1)}, u32[]{:S(2)}, u32[]{:S(2)}) async-start(bf16[2,32,6]{2,0,1:T(2,128)(2,1)} %copy.42), calls=%async_computation | async-start | bytes 32768 | tf_op jit(solution)/shard_map/all_to_all | solution.py:89
  23.5 2.6 gather_fusion.3
  26.1 2.3 reshape.357
  28.4 2.6 gather_fusion.2
  31.0 2.3 reshape.349
  33.3 4.6 broadcast_select_fusion
  37.9 3.3 copy.46
  41.2 9.8 %all-to-all-start.3 = ((bf16[2,32,6,2560]{3,0,2,1:T(2,128)(2,1)}), bf16[2,32,6,2560]{3,0,2,1:T(2,128)(2,1)S(1)}, u32[]{:S(2)}, u32[]{:S(2)}) async-start(bf16[2,32,6,2560]{3,0,2,1:T(2,128)(2,1)} %copy.46), calls=%async_computation.3 | async-start | bytes 3932160 | tf_op jit(solution)/shard_map/all_to_all | solution.py:89
  51.0 5.0 copy.43
  56.0 42.2 %all-to-all-done.3 = bf16[2,32,6,2560]{3,0,2,1:T(2,128)(2,1)S(1)} async-done(((bf16[2,32,6,2560]{3,0,2,1:T(2,128)(2,1)}), bf16[2,32,6,2560]{3,0,2,1:T(2,128)(2,1)S(1)}, u32[]{:S(2)}, u32[]{:S(2)}) %all-to-all-start.3) | async-done | bytes 1966112 | tf_op jit(solution)/shard_map/all_to_all | solution.py:89
  98.2 6.5 %all-to-all-start.1 = ((bf16[2,32,6,2560]{3,0,2,1:T(2,128)(2,1)}), bf16[2,32,6,2560]{3,0,2,1:T(2,128)(2,1)}, u32[]{:S(2)}, u32[]{:S(2)}) async-start(bf16[2,32,6,2560]{3,0,2,1:T(2,128)(2,1)} %copy.43), calls=%async_computation.1 | async-start | bytes 3932160 | tf_op jit(solution)/shard_map/all_to_all | solution.py:89
  109.0 9.6 %slice_reduce_fusion.1 = (bf16[32,6,2560]{2,1,0:T(8,128)(2,1)}, bf16[32,6,2560]{2,1,0:T(8,128)(2,1)}) fusion(bf16[2,32,6,2560]{3,0,2,1:T(2,128)(2,1)S(1)} %all-to-all-done.3), kind=kLoop, calls=%fused_computation.32 | loop fusion | bytes 3932160 | tf_op jit(solution)/shard_map/slice | solution.py:100
  120.1 23.3 %all-to-all-done.1 = bf16[2,32,6,2560]{3,0,2,1:T(2,128)(2,1)} async-done(((bf16[2,32,6,2560]{3,0,2,1:T(2,128)(2,1)}), bf16[2,32,6,2560]{3,0,2,1:T(2,128)(2,1)}, u32[]{:S(2)}, u32[]{:S(2)}) %all-to-all-start.1) | async-done | bytes 1966112 | tf_op jit(solution)/shard_map/all_to_all | solution.py:89
  143.4 11.5 %slice_reduce_fusion.3 = (bf16[32,6,2560]{2,1,0:T(8,128)(2,1)}, bf16[32,6,2560]{2,1,0:T(8,128)(2,1)}) fusion(bf16[2,32,6,2560]{3,0,2,1:T(2,128)(2,1)} %all-to-all-done.1), kind=kLoop, calls=%fused_computation.34 | loop fusion | bytes 3932160 | tf_op jit(solution)/shard_map/slice | solution.py:100
  157.9 3.1 fusion.26
  162.3 73.3 %collective-permute-done.1 = bf16[1,2560,384]{2,1,0:T(8,128)(2,1)} collective-permute-done((bf16[1,2560,384]{2,1,0:T(8,128)(2,1)}, bf16[1,2560,384]{2,1,0:T(8,128)(2,1)}, u32[]{:S(2)}, u32[]{:S(2)}) %collective-permute-start.1) | collective-permute-done | bytes 1966112 | tf_op jit(solution)/shard_map/ppermute | solution.py:15
  235.7 2.2 fusion.13
  237.9 2.4 fusion.31
  240.2 37.5 %collective-permute-done = bf16[1,2560,384]{2,1,0:T(8,128)(2,1)} collective-permute-done((bf16[1,2560,384]{2,1,0:T(8,128)(2,1)}, bf16[1,2560,384]{2,1,0:T(8,128)(2,1)}, u32[]{:S(2)}, u32[]{:S(2)}) %collective-permute-start) | collective-permute-done | bytes 1966112 | tf_op jit(solution)/shard_map/ppermute | solution.py:15
  277.8 3.0 multiply_convert_fusion.1
  281.5 3.2 convolution_convert_fusion.6
  284.6 2.2 stack.34
  286.9 2.2 squeeze.44
  289.1 2.9 multiply_convert_fusion.2
  293.7 2.4 stack.33
  296.1 2.4 pad_maximum_fusion
  298.5 3.3 copy.44
  301.8 9.5 %all-to-all-start.2 = ((bf16[2,32,6,2560]{3,0,2,1:T(2,128)(2,1)}), bf16[2,32,6,2560]{3,0,2,1:T(2,128)(2,1)}, u32[]{:S(2)}, u32[]{:S(2)}) async-start(bf16[2,32,6,2560]{3,0,2,1:T(2,128)(2,1)} %copy.44), calls=%async_computation.2 | async-start | bytes 3932160 | tf_op jit(solution)/shard_map/all_to_all | solution.py:117
  311.3 2.5 fusion.11
  313.8 3.4 fusion.4
  317.2 2.2 stack.37
  319.4 2.5 fusion.24
  323.8 2.2 stack.36
  326.0 2.4 pad_maximum_fusion.1
  328.4 3.3 copy.47
  331.8 26.7 %all-to-all-done.2 = bf16[2,32,6,2560]{3,0,2,1:T(2,128)(2,1)} async-done(((bf16[2,32,6,2560]{3,0,2,1:T(2,128)(2,1)}), bf16[2,32,6,2560]{3,0,2,1:T(2,128)(2,1)}, u32[]{:S(2)}, u32[]{:S(2)}) %all-to-all-start.2) | async-done | bytes 1966112 | tf_op jit(solution)/shard_map/all_to_all | solution.py:117
  358.5 6.0 %all-to-all-start.4 = ((bf16[2,32,6,2560]{3,0,2,1:T(2,128)(2,1)}), bf16[2,32,6,2560]{3,0,2,1:T(2,128)(2,1)}, u32[]{:S(2)}, u32[]{:S(2)}) async-start(bf16[2,32,6,2560]{3,0,2,1:T(2,128)(2,1)} %copy.47), calls=%async_computation.4 | async-start | bytes 3932160 | tf_op jit(solution)/shard_map/all_to_all | solution.py:118
  364.5 2.9 convolution_convert_fusion
  369.3 2.1 convolution_convert_fusion.4
  371.7 2.2 convolution_convert_fusion.2
  376.1 72.3 %collective-permute-done.5 = bf16[384,2560]{1,0:T(8,128)(2,1)} collective-permute-done((bf16[384,2560]{1,0:T(8,128)(2,1)}, bf16[384,2560]{1,0:T(8,128)(2,1)}, u32[]{:S(2)}, u32[]{:S(2)}) %collective-permute-start.5) | collective-permute-done | bytes 1966112 | tf_op jit(solution)/shard_map/ppermute | solution.py:15
  448.4 3.5 fusion.7
  451.9 38.6 %collective-permute-done.3 = bf16[2560,384]{1,0:T(8,128)(2,1)} collective-permute-done((bf16[2560,384]{1,0:T(8,128)(2,1)}, bf16[2560,384]{1,0:T(8,128)(2,1)}, u32[]{:S(2)}, u32[]{:S(2)}) %collective-permute-start.3) | collective-permute-done | bytes 1966112 | tf_op jit(solution)/shard_map/ppermute | solution.py:15
  490.5 3.7 fusion.5
  494.2 38.4 %collective-permute-done.4 = bf16[2560,384]{1,0:T(8,128)(2,1)} collective-permute-done((bf16[2560,384]{1,0:T(8,128)(2,1)}, bf16[2560,384]{1,0:T(8,128)(2,1)}, u32[]{:S(2)}, u32[]{:S(2)}) %collective-permute-start.4) | collective-permute-done | bytes 1966112 | tf_op jit(solution)/shard_map/ppermute | solution.py:15
  532.6 3.7 fusion.6
  544.2 2.7 convolution_convert_fusion.9
  (90 shorter events, 34.9 us)
Async XLA Ops:
  0.6 22.9 %copy-start = (bf16[16,2560]{1,0:T(8,128)(2,1)S(1)}, bf16[16,2560]{1,0:T(8,128)(2,1)}, u32[]{:S(2)}) copy-start(bf16[16,2560]{1,0:T(8,128)(2,1)} %param.10) | copy-start | bytes 245764
  10.7 30.4 %all-to-all-start = ((bf16[2,32,6]{2,0,1:T(2,128)(2,1)}), bf16[2,32,6]{2,0,1:T(2,128)(2,1)S(1)}, u32[]{:S(2)}, u32[]{:S(2)}) async-start(bf16[2,32,6]{2,0,1:T(2,128)(2,1)} %copy.42), calls=%async_computation | async-start | bytes 32768 | tf_op jit(solution)/shard_map/all_to_all | solution.py:89
  26.1 2.3 copy-start.2
  41.2 57.1 %all-to-all-start.3 = ((bf16[2,32,6,2560]{3,0,2,1:T(2,128)(2,1)}), bf16[2,32,6,2560]{3,0,2,1:T(2,128)(2,1)S(1)}, u32[]{:S(2)}, u32[]{:S(2)}) async-start(bf16[2,32,6,2560]{3,0,2,1:T(2,128)(2,1)} %copy.46), calls=%async_computation.3 | async-start | bytes 3932160 | tf_op jit(solution)/shard_map/all_to_all | solution.py:89
  98.2 45.1 %all-to-all-start.1 = ((bf16[2,32,6,2560]{3,0,2,1:T(2,128)(2,1)}), bf16[2,32,6,2560]{3,0,2,1:T(2,128)(2,1)}, u32[]{:S(2)}, u32[]{:S(2)}) async-start(bf16[2,32,6,2560]{3,0,2,1:T(2,128)(2,1)} %copy.43), calls=%async_computation.1 | async-start | bytes 3932160 | tf_op jit(solution)/shard_map/all_to_all | solution.py:89
  104.7 133.2 %collective-permute-start.2 = (bf16[1,384,2560]{2,1,0:T(8,128)(2,1)}, bf16[1,384,2560]{2,1,0:T(8,128)(2,1)}, u32[]{:S(2)}, u32[]{:S(2)}) collective-permute-start(bf16[1,384,2560]{2,1,0:T(8,128)(2,1)} %param.17), channel_id=1, source_target_pairs={{0,32},{32,64},{64,96},{96,128},{128,160},{160,192},{192,224},{224... | collective-permute-start | bytes 5898248 | tf_op jit(solution)/shard_map/ppermute | solution.py:15
  105.8 129.9 %collective-permute-start.1 = (bf16[1,2560,384]{2,1,0:T(8,128)(2,1)}, bf16[1,2560,384]{2,1,0:T(8,128)(2,1)}, u32[]{:S(2)}, u32[]{:S(2)}) collective-permute-start(bf16[1,2560,384]{2,1,0:T(8,128)(2,1)} %param.16), channel_id=1, source_target_pairs={{0,32},{32,64},{64,96},{96,128},{128,160},{160,192},{192,224},{224... | collective-permute-start | bytes 5898248 | tf_op jit(solution)/shard_map/ppermute | solution.py:15
  107.3 170.5 %collective-permute-start = (bf16[1,2560,384]{2,1,0:T(8,128)(2,1)}, bf16[1,2560,384]{2,1,0:T(8,128)(2,1)}, u32[]{:S(2)}, u32[]{:S(2)}) collective-permute-start(bf16[1,2560,384]{2,1,0:T(8,128)(2,1)} %param.15), channel_id=1, source_target_pairs={{0,32},{32,64},{64,96},{96,128},{128,160},{160,192},{192,224},{224... | collective-permute-start | bytes 5898248 | tf_op jit(solution)/shard_map/ppermute | solution.py:15
  157.9 3.1 copy-start.3
  280.8 0.6 copy-start.11
  289.1 2.9 copy-start.7
  301.8 56.7 %all-to-all-start.2 = ((bf16[2,32,6,2560]{3,0,2,1:T(2,128)(2,1)}), bf16[2,32,6,2560]{3,0,2,1:T(2,128)(2,1)}, u32[]{:S(2)}, u32[]{:S(2)}) async-start(bf16[2,32,6,2560]{3,0,2,1:T(2,128)(2,1)} %copy.44), calls=%async_computation.2 | async-start | bytes 3932160 | tf_op jit(solution)/shard_map/all_to_all | solution.py:117
  311.3 2.5 copy-start.9
  319.4 2.5 copy-start.4
  358.5 181.8 %all-to-all-start.4 = ((bf16[2,32,6,2560]{3,0,2,1:T(2,128)(2,1)}), bf16[2,32,6,2560]{3,0,2,1:T(2,128)(2,1)}, u32[]{:S(2)}, u32[]{:S(2)}) async-start(bf16[2,32,6,2560]{3,0,2,1:T(2,128)(2,1)} %copy.47), calls=%async_computation.4 | async-start | bytes 3932160 | tf_op jit(solution)/shard_map/all_to_all | solution.py:118
  364.5 4.8 copy-start.10
  367.4 4.3 copy-start.8
  367.4 81.0 %collective-permute-start.5 = (bf16[384,2560]{1,0:T(8,128)(2,1)}, bf16[384,2560]{1,0:T(8,128)(2,1)}, u32[]{:S(2)}, u32[]{:S(2)}) collective-permute-start(bf16[384,2560]{1,0:T(8,128)(2,1)} %convolution_convert_fusion), channel_id=1, source_target_pairs={{0,224},{32,0},{64,32},{96,64},{128,96},{160,128},{192,160},{224,1... | collective-permute-start | bytes 5898248 | tf_op jit(solution)/shard_map/ppermute | solution.py:15
  371.4 76.9 %copy-start.6 = (bf16[192,2560]{1,0:T(8,128)(2,1)S(1)}, bf16[192,2560]{1,0:T(8,128)(2,1)}, u32[]{:S(2)}) copy-start(bf16[192,2560]{1,0:T(8,128)(2,1)} %squeeze.44) | copy-start | bytes 2949124
  371.4 119.1 %collective-permute-start.3 = (bf16[2560,384]{1,0:T(8,128)(2,1)}, bf16[2560,384]{1,0:T(8,128)(2,1)}, u32[]{:S(2)}, u32[]{:S(2)}) collective-permute-start(bf16[2560,384]{1,0:T(8,128)(2,1)} %convolution_convert_fusion.4), channel_id=1, source_target_pairs={{0,224},{32,0},{64,32},{96,64},{128,96},{160,128},{192,160},{224,1... | collective-permute-start | bytes 5898248 | tf_op jit(solution)/shard_map/ppermute | solution.py:15
  373.8 158.8 %collective-permute-start.4 = (bf16[2560,384]{1,0:T(8,128)(2,1)}, bf16[2560,384]{1,0:T(8,128)(2,1)}, u32[]{:S(2)}, u32[]{:S(2)}) collective-permute-start(bf16[2560,384]{1,0:T(8,128)(2,1)} %convolution_convert_fusion.2), channel_id=1, source_target_pairs={{0,224},{32,0},{64,32},{96,64},{128,96},{160,128},{192,160},{224,1... | collective-permute-start | bytes 5898248 | tf_op jit(solution)/shard_map/ppermute | solution.py:15
  542.1 5.8 %copy-start.1 = (bf16[16,2560]{1,0:T(8,128)(2,1)S(1)}, bf16[16,2560]{1,0:T(8,128)(2,1)}, u32[]{:S(2)}) copy-start(bf16[16,2560]{1,0:T(8,128)(2,1)} %param.10) | copy-start | bytes 245764
  544.2 2.7 copy-start.5
where the time goes:
time: 558 us; the launch traced here: 548 us
  waiting for transfers between devices  352 us (63%)
  local copies, waits for them, and re-layouts  78.5 us (14%)
  starting transfers between devices  52 us (9%)
  matrix products  51.9 us (9%)
  other arithmetic  12.1 us (2%)
    ppermute x6, waiting for transfers between devices, passed_along(): lax.ppermute(x, axis, [(i, (i + by) % length) for i in range(length)])  260 us
    all_to_all x3, waiting for transfers between devices, shards(): lax.all_to_all(for_sending((outgoing_input, send_dy, send_gate)), 'dev',...  65.5 us
    all_to_all x3, starting transfers between devices, shards(): lax.all_to_all(for_sending((outgoing_input, send_dy, send_gate)), 'dev',...  28.8 us
    all_to_all x1, waiting for transfers between devices, shards(): lax.all_to_all(back_out, 'dev', split_axis=1, concat_axis=1, tiled=True)  26.7 us
    slice x1, local copies, waits for them, and re-layouts, shards(): recv_x[0]  11.5 us
  transfers between devices with their start and end apart: 11, of which 8 were waited for; matrix products, arithmetic and copies ran while one was open for 18% of the time, Pallas kernels for 0%

commit v1 on v0

v1 whole, which is shorter than its diff:
```python
import jax
import jax.numpy as jnp
from jax import lax
from jax.experimental import pallas as pl
from jax.experimental.pallas import tpu as pltpu
from jax.sharding import PartitionSpec as P

BF = jnp.bfloat16
F32 = jnp.float32
D = 2560
H = 384
ROWS = 16
CAP = 6
NX, NY, NZ = 4, 4, 8
META = 128
GATE_LANE = 64
BLK = NZ * CAP
HALF = NX * BLK
ALL = 2 * HALF
TOK = NZ * ROWS
STEP = 512
MESH = pl.DeviceIdType.MESH


def nn(a, b):
    return lax.dot_general(a, b, (((1,), (0,)), ((), ())), preferred_element_type=F32)


def nt(a, b):
    return lax.dot_general(a, b, (((1,), (1,)), ((), ())), preferred_element_type=F32)


def tn(a, b):
    return lax.dot_general(a, b, (((0,), (0,)), ((), ())), preferred_element_type=F32)


def rows(i, n):
    return pl.ds(pl.multiple_of(i * n, n), n)


def over_lanes(body):
    def run(i, carry):
        body(pl.ds(pl.multiple_of(i * STEP, STEP), STEP))
        return carry

    lax.fori_loop(0, D // STEP, run, 0)


def kernel(
    tokens, grad_out, meta_in, wg_hbm, wu_hbm, wd_hbm,
    mixed, token_grad, gg_hbm, gu_hbm, gd_hbm,
    bx, bdy, sx, sdy, rx, rdy, wg, wu, wd, sel, sel_gate,
    act, slope, hid, gpre, part, out_far, dx_far, out_in, dx_in,
    out_back, dx_back, out_got, dx_got, pout, pdx, zout, zdx, gg, gu, gd,
    w_sem, z_send, z_recv, x_send, x_recv, c_send, c_recv,
    e_send, e_recv, b_send, b_recv, p_send, p_recv, g_sem,
):
    g = lax.axis_index("group")
    d = lax.axis_index("dev")
    y, z_lo = g // 2, g % 2
    z_hi, x, c = d // 8, (d // 2) % 4, d % 2
    z = z_hi * 2 + z_lo

    def device(x_, y_, z_, c_):
        return (y_ * 2 + z_ % 2, ((z_ // 2) * NX + x_) * 2 + c_)

    y_prev = jnp.where(z_lo == 1, y, (y + NY - 1) % NY)
    y_next = jnp.where(z_lo == 0, y, (y + 1) % NY)

    def z_taker(k):
        return device(x, y if k % 2 == 0 else y_prev, (z + k) % NZ, c)

    def z_owner(k):
        return device(x, y if k % 2 == 0 else y_next, (z + k) % NZ, c)

    sibling = device(x, y, z, 1 - c)

    w_copies = [
        pltpu.make_async_copy(src.at[0], dst, w_sem.at[i])
        for i, (src, dst) in enumerate(((wg_hbm, wg), (wu_hbm, wu), (wd_hbm, wd)))
    ]
    for copy in w_copies:
        copy.start()

    barrier = pltpu.get_barrier_semaphore()
    near = [z_taker(k) for k in range(1, NZ)] + [z_owner(k) for k in range(1, NZ, 2)]
    near += [device((x + k) % NX, y, z, c) for k in range(1, NX)] + [sibling]
    for other in near:
        pl.semaphore_signal(barrier, inc=1, device_id=other, device_id_type=MESH)
    mine = rows(z, ROWS)
    bx[mine, :D] = tokens[...]
    bx[mine, D:] = meta_in[...]
    bdy[mine, :] = grad_out[...]
    pl.semaphore_wait(barrier, len(near))

    sent = []

    def send(src, dst, s_sem, r_sem, to):
        copy = pltpu.make_async_remote_copy(
            src_ref=src, dst_ref=dst, send_sem=s_sem, recv_sem=r_sem,
            device_id=to, device_id_type=MESH,
        )
        copy.start()
        sent.append(copy)

    def arrived(dst, s_sem, r_sem):
        pltpu.make_async_remote_copy(
            src_ref=dst, dst_ref=dst, send_sem=s_sem, recv_sem=r_sem,
            device_id=sibling, device_id_type=MESH,
        ).wait_recv()

    far_first = (4, 3, 5, 2, 6, 1, 7)
    for s, buf in enumerate((bx, bdy)):
        for k in far_first:
            send(buf.at[mine], buf.at[mine], z_send.at[s, k], z_recv.at[s, z], z_taker(k))

    def z_arrived(s, buf):
        for k in range(1, NZ):
            zz = (z + k) % NZ
            arrived(buf.at[rows(zz, ROWS)], z_send.at[s, 0], z_recv.at[s, zz])

    z_arrived(0, bx)
    meta = bx[:, D:].astype(F32)
    lane = lax.broadcasted_iota(jnp.int32, (TOK, META), 1)
    gate_at = pltpu.roll(meta, GATE_LANE, 1)
    first = (g * 16 + z_hi * NX).astype(F32)
    hits, gate_of = [], []
    hit_all = jnp.zeros((TOK, META), F32)
    for j in range(NX):
        match = jnp.where((meta == first + j) & (lane < 6), 1.0, 0.0)
        hits.append(jnp.sum(match, axis=1, keepdims=True))
        gate_of.append(jnp.sum(match * gate_at, axis=1, keepdims=True))
        hit_all = hit_all + jnp.where(lane == j, hits[j], 0.0)
    t_row = lax.broadcasted_iota(jnp.int32, (TOK, TOK), 0)
    t_col = lax.broadcasted_iota(jnp.int32, (TOK, TOK), 1)
    before = jnp.where((t_col < t_row) & (t_col // ROWS == t_row // ROWS), 1.0, 0.0)
    rank_all = nn(before.astype(BF), hit_all.astype(BF))
    q = lax.broadcasted_iota(jnp.int32, (TOK, HALF), 1)
    block = lax.broadcasted_iota(jnp.int32, (TOK, HALF), 0) // ROWS
    place = jnp.zeros((TOK, HALF), F32)
    hit_q = jnp.zeros((TOK, HALF), F32)
    gate_q = jnp.zeros((TOK, HALF), F32)
    for j in range(NX):
        rank = jnp.sum(jnp.where(lane == j, rank_all, 0.0), axis=1, keepdims=True)
        inside = (q >= j * BLK) & (q < (j + 1) * BLK)
        place = jnp.where(inside, rank + j * BLK, place)
        hit_q = jnp.where(inside, hits[j], hit_q)
        gate_q = jnp.where(inside, gate_of[j], gate_q)
    placed = place + (block * CAP).astype(F32) == q.astype(F32)
    chosen = jnp.where(placed, hit_q, 0.0)
    sel[...] = chosen.astype(BF)
    sel_gate[...] = (chosen * gate_q).astype(BF)

    my_slot = rows(c * NX + x, BLK)

    def dispatch(s, selector, buf, out, got):
        def body(at):
            out[:, at] = tn(selector[...], buf[:, at]).astype(BF)

        over_lanes(body)
        for k in (2, 1, 3):
            j = (x + k) % NX
            send(out.at[rows(j, BLK)], got.at[my_slot], x_send.at[s, k], x_recv.at[s, x], device(j, y, z, c))
        got[my_slot, :] = out[rows(x, BLK), :]
        send(got.at[my_slot], got.at[my_slot], c_send.at[s, 0], c_recv.at[s, x], sibling)

    def share(s, got):
        for k in (1, 3, 2):
            j = (x + k) % NX
            slot = got.at[rows(c * NX + j, BLK)]
            arrived(slot, x_send.at[s, 0], x_recv.at[s, j])
            send(slot, slot, c_send.at[s, k], c_recv.at[s, j], sibling)

    def shared(s, got):
        for k in range(NX):
            j = (x + k) % NX
            arrived(got.at[rows((1 - c) * NX + j, BLK)], c_send.at[s, 0], c_recv.at[s, j])

    dispatch(0, sel, bx, sx, rx)
    z_arrived(1, bdy)
    dispatch(1, sel_gate, bdy, sdy, rdy)
    share(0, rx)
    shared(0, rx)

    far_rows, own_rows = rows(1 - c, HALF), rows(c, HALF)

    w_copies[0].wait()
    w_copies[1].wait()
    pre_gate = nn(rx[...], wg[...])
    pre_up = nn(rx[...], wu[...])
    sig = jax.nn.sigmoid(pre_gate)
    silu = pre_gate * sig
    act[...] = silu
    slope[...] = pre_up * sig * (1.0 + pre_gate * (1.0 - sig))
    hid[...] = (silu * pre_up).astype(BF)
    w_copies[2].wait()

    def back(s, rows_of, far, near_in, summed, got):
        def body_far(at):
            far[:, at] = rows_of(far_rows, at).astype(BF)

        over_lanes(body_far)
        send(far, near_in, e_send.at[s], e_recv.at[s], sibling)

        def body_own(at):
            part[:, at] = rows_of(own_rows, at)

        over_lanes(body_own)

    def give_back(s, near_in, summed, got):
        arrived(near_in, e_send.at[s], e_recv.at[s])
        summed[...] = (part[...] + near_in[...].astype(F32)).astype(BF)
        for k in (2, 1, 3):
            j = (x + k) % NX
            send(summed.at[rows(j, BLK)], got.at[rows(x, BLK)], b_send.at[s, k], b_recv.at[s, x], device(j, y, z, c))
        got[rows(x, BLK), :] = summed[rows(x, BLK), :]

    def combine(s, selector, got, partial, landed):
        for k in range(1, NX):
            j = (x + k) % NX
            arrived(got.at[rows(j, BLK)], b_send.at[s, 0], b_recv.at[s, j])

        def body(at):
            partial[:, at] = nn(selector[...], got[:, at]).astype(BF)

        over_lanes(body)
        for k in far_first:
            send(partial.at[rows((z + k) % NZ, ROWS)], landed.at[mine], p_send.at[s, k], p_recv.at[s, z], z_owner(k))
        landed[mine, :] = partial[mine, :]

    def finish(s, landed, result):
        for k in range(1, NZ):
            zz = (z + k) % NZ
            arrived(landed.at[rows(zz, ROWS)], p_send.at[s, 0], p_recv.at[s, zz])
        total = landed[:ROWS, :].astype(F32)
        for i in range(1, NZ):
            total = total + landed[i * ROWS:(i + 1) * ROWS, :].astype(F32)
        result[...] = total.astype(BF)

    back(0, lambda r, at: nn(hid[r, :], wd[:, at]), out_far, out_in, out_back, out_got)
    share(1, rdy)
    give_back(0, out_in, out_back, out_got)
    shared(1, rdy)

    back_hidden = nt(rdy[...], wd[...])
    gpre[:, :H] = (back_hidden * slope[...]).astype(BF)
    gpre[:, H:] = (back_hidden * act[...]).astype(BF)
    back(
        1,
        lambda r, at: nt(gpre[r, :H], wg[at, :]) + nt(gpre[r, H:], wu[at, :]),
        dx_far, dx_in, dx_back, dx_got,
    )
    combine(0, sel_gate, out_got, pout, zout)
    give_back(1, dx_in, dx_back, dx_got)

    def grads_in(at):
        both = tn(rx[:, at], gpre[...])
        gg[at, :] = both[:, :H].astype(BF)
        gu[at, :] = both[:, H:].astype(BF)

    over_lanes(grads_in)

    def grads_down(at):
        gd[:, at] = tn(hid[...], rdy[:, at]).astype(BF)

    over_lanes(grads_down)
    g_copies = [
        pltpu.make_async_copy(src, dst.at[0], g_sem.at[i])
        for i, (src, dst) in enumerate(((gg, gg_hbm), (gu, gu_hbm), (gd, gd_hbm)))
    ]
    for copy in g_copies:
        copy.start()
    combine(1, sel, dx_got, pdx, zdx)
    finish(0, zout, mixed)
    finish(1, zdx, token_grad)
    for copy in sent:
        copy.wait_send()
    for copy in g_copies:
        copy.wait()


def shards(tokens, grad_out, routes, gates, pull_list, counts, w_gate, w_up, w_down):
    g = lax.axis_index("group")
    d = lax.axis_index("dev")
    n_pull = pull_list.shape[1]
    mine = jnp.arange(pull_list.shape[0]) == g
    pull_row = jnp.sum(jnp.where(mine[:, None], pull_list, 0), axis=0)
    count = jnp.sum(jnp.where(mine, counts, 0))
    pulled = routes[:, :, None] == 16 + jnp.arange(n_pull)[None, None, :]
    expert = jnp.where(
        routes < 16, g * 16 + routes, jnp.sum(jnp.where(pulled, pull_row[None, None, :], 0), axis=2)
    )
    alive = d * ROWS + jnp.arange(ROWS) < count
    expert = jnp.where(alive[:, None], expert, -1)
    gap = jnp.zeros((ROWS, GATE_LANE - routes.shape[1]), BF)
    meta = jnp.concatenate([expert.astype(BF), gap, gates, gap], axis=1)

    vmem = pl.BlockSpec(memory_space=pltpu.VMEM)
    hbm = pl.BlockSpec(memory_space=pl.ANY)
    dma = pltpu.SemaphoreType.DMA
    return pl.pallas_call(
        kernel,
        out_shape=(
            jax.ShapeDtypeStruct((ROWS, D), BF),
            jax.ShapeDtypeStruct((ROWS, D), BF),
            jax.ShapeDtypeStruct((1, D, H), BF),
            jax.ShapeDtypeStruct((1, D, H), BF),
            jax.ShapeDtypeStruct((1, H, D), BF),
        ),
        in_specs=[vmem] * 3 + [hbm] * 3,
        out_specs=(vmem, vmem, hbm, hbm, hbm),
        scratch_shapes=[
            pltpu.VMEM((TOK, D + META), BF),
            pltpu.VMEM((TOK, D), BF),
            pltpu.VMEM((HALF, D), BF),
            pltpu.VMEM((HALF, D), BF),
            pltpu.VMEM((ALL, D), BF),
            pltpu.VMEM((ALL, D), BF),
            pltpu.VMEM((D, H), BF),
            pltpu.VMEM((D, H), BF),
            pltpu.VMEM((H, D), BF),
            pltpu.VMEM((TOK, HALF), BF),
            pltpu.VMEM((TOK, HALF), BF),
            pltpu.VMEM((ALL, H), F32),
            pltpu.VMEM((ALL, H), F32),
            pltpu.VMEM((ALL, H), BF),
            pltpu.VMEM((ALL, 2 * H), BF),
            pltpu.VMEM((HALF, D), F32),
            pltpu.VMEM((HALF, D), BF),
            pltpu.VMEM((HALF, D), BF),
            pltpu.VMEM((HALF, D), BF),
            pltpu.VMEM((HALF, D), BF),
            pltpu.VMEM((HALF, D), BF),
            pltpu.VMEM((HALF, D), BF),
            pltpu.VMEM((HALF, D), BF),
            pltpu.VMEM((HALF, D), BF),
            pltpu.VMEM((TOK, D), BF),
            pltpu.VMEM((TOK, D), BF),
            pltpu.VMEM((TOK, D), BF),
            pltpu.VMEM((TOK, D), BF),
            pltpu.VMEM((D, H), BF),
            pltpu.VMEM((D, H), BF),
            pltpu.VMEM((H, D), BF),
            dma((3,)),
            dma((2, NZ)),
            dma((2, NZ)),
            dma((2, NX)),
            dma((2, NX)),
            dma((2, NX)),
            dma((2, NX)),
            dma((2,)),
            dma((2,)),
            dma((2, NX)),
            dma((2, NX)),
            dma((2, NZ)),
            dma((2, NZ)),
            dma((3,)),
        ],
        compiler_params=pltpu.CompilerParams(
            collective_id=0, has_side_effects=True, vmem_limit_bytes=56 * 1024 * 1024
        ),
    )(tokens, grad_out, meta, w_gate, w_up, w_down)


def solution(mesh):
    both = ("group", "dev")
    in_specs = (
        P(both, None), P(both, None), P(both, None), P(both, None), P(), P(),
        P(both, None, None), P(both, None, None), P(both, None, None),
    )
    out_specs = (
        P(both, None), P(both, None),
        P(both, None, None), P(both, None, None), P(both, None, None),
    )
    return jax.shard_map(shards, mesh=mesh, in_specs=in_specs, out_specs=out_specs, check_vma=False)
```

time: 558 us -> 119 us (0.21); the launches traced: 548 us -> 118 us
  waiting for transfers between devices: 352 us -> 0 us
  Pallas kernels: 0 us -> 102 us
  local copies, waits for them, and re-layouts: 78.5 us -> 11.4 us
  starting transfers between devices: 52 us -> 0 us
  matrix products: 51.9 us -> 0 us
  other arithmetic: 12.1 us -> 4.25 us
    ppermute x6 -> x0, waiting for transfers between devices: 260 us -> none  [passed_along(): lax.ppermute(x, axis, [(i, (i + by) % length) for i in range(length)])]
    pallas_call x0 -> x1, Pallas kernels: none -> 102 us  [shards(): pl.pallas_call(kernel, out_shape=(jax.ShapeDtypeStruct((ROWS, D), BF), ja...]
    all_to_all x5 -> x0, waiting for transfers between devices: 92.3 us -> none  [the longest x3 65.5 us: shards(): lax.all_to_all(for_sending((outgoing_input, send_dy, send_gate)), 'dev',...]
    dot_general x20 -> x0, matrix products: 51.9 us -> none  [the longest x2 6.43 us: expert_pass(): jnp.dot(gated_hidden.T, rows_dy, preferred_element_type=jnp.float32)]
    all_to_all x5 -> x0, starting transfers between devices: 44.3 us -> none  [the longest x3 28.8 us: shards(): lax.all_to_all(for_sending((outgoing_input, send_dy, send_gate)), 'dev',...]
    slice x2 -> x0, local copies, waits for them, and re-layouts: 21.2 us -> none  [the longest x1 11.5 us: shards(): recv_x[0]]
    another operation x6 -> x0, local copies, waits for them, and re-layouts: 15.7 us -> none  [the longest x3 7.93 us: shards(): jnp.stack([owned[0], far_out]).reshape(2, dev_count, capacity, width)]
    gather x7 -> x0, local copies, waits for them, and re-layouts: 13.2 us -> none  [the longest x2 4.89 us: shards(): outgoing_input = jnp.where(present[..., None], tokens[token_of], zero_value)]
  transfers between devices with their start and end apart: 11 -> 0, of which waited for: 8 -> 0; matrix products, arithmetic and copies ran while one was open for 18% -> 0% of each run, Pallas kernels for 0% -> 0%
where the time goes in v1:
time: 119 us; the launch traced here: 118 us
  Pallas kernels  102 us (86%)
  local copies, waits for them, and re-layouts  11.4 us (10%)
  other arithmetic  4.25 us (4%)
    pallas_call x1, Pallas kernels, shards(): pl.pallas_call(kernel, out_shape=(jax.ShapeDtypeStruct((ROWS, D), BF), ja...  102 us
    unnamed x11, local copies, waits for them, and re-layouts  11.3 us

profile of v1, /device:TPU:1, one launch (start us, length us, event | category | flops | bytes accessed | tf_op | source)
XLA Modules:
  0.0 118.2 jit_solution(4642418415927641786)
XLA Ops:
  0.6 1.3 %select_reduce_fusion.2 = s32[]{:T(128)} fusion(s32[8]{0:T(128)} %param.14, s32[]{:T(128)S(6)} %axis_index.25), kind=kLoop, calls=%fused_computation.5 | loop fusion | flops 23 | bytes 40 | tf_op jit(solution)/shard_map/reduce_sum | solution.py:288
  1.9 0.7 add_compare_fusion
  2.6 0.8 select_reduce_fusion.1
  3.4 0.8 select_reduce_fusion
  4.1 0.1 copy.20
  4.2 0.8 copy.21
  5.0 0.8 copy.18
  5.8 0.1 select_convert_fusion
  5.8 0.7 pad_maximum_fusion.meta_in
  6.5 102.0 %shard_map.128 = (bf16[16,2560]{1,0:T(8,128)(2,1)}, bf16[16,2560]{1,0:T(8,128)(2,1)}, bf16[1,2560,384]{2,1,0:T(8,128)(2,1)}, bf16[1,2560,384]{2,1,0:T(8,128)(2,1)}, bf16[1,384,2560]{2,1,0:T(8,128)(2,1)}) custom-call(bf16[16,2560]{1,0:T(8,128)(2,1)} %tokens.1, bf16[16,2560]{1,0:T(8,128)(2,1)} %grad_out.1, bf16[16,128]{1,0:T(8,128)(2,1)} %pad_maximum_fusion.meta_in, ...), custom_call_target="tpu_custom_call" | custom-call | tf_op jit(solution)/shard_map/pallas_call | solution.py:301
  108.5 1.5 %copy.27 = bf16[16,2560]{1,0:T(8,128)(2,1)} copy(bf16[16,2560]{1,0:T(8,128)(2,1)} %get-tuple-element.10) | data formatting | bytes 163840
  110.0 1.5 %copy.28 = bf16[16,2560]{1,0:T(8,128)(2,1)} copy(bf16[16,2560]{1,0:T(8,128)(2,1)} %get-tuple-element.11) | data formatting | bytes 163840
  111.5 0.0 copy-start.1
  111.6 3.2 %copy.29 = bf16[1,2560,384]{2,1,0:T(8,128)(2,1)} copy(bf16[1,2560,384]{2,1,0:T(8,128)(2,1)} %get-tuple-element.12) | data formatting | bytes 3932160
  114.7 0.0 copy-done.1
  114.7 0.0 copy-start
  114.7 1.3 %copy.30 = bf16[1,2560,384]{2,1,0:T(8,128)(2,1)} copy(bf16[1,2560,384]{2,1,0:T(8,128)(2,1)S(1)} %copy-done.1) | data formatting | bytes 3932160
  116.0 1.0 copy-done
  117.0 1.3 %copy.31 = bf16[1,384,2560]{2,1,0:T(8,128)(2,1)} copy(bf16[1,384,2560]{2,1,0:T(8,128)(2,1)S(1)} %copy-done) | data formatting | bytes 3932160
  (3 shorter events, 0.0 us)
Async XLA Ops:
  111.5 3.2 %copy-start.1 = (bf16[1,2560,384]{2,1,0:T(8,128)(2,1)S(1)}, bf16[1,2560,384]{2,1,0:T(8,128)(2,1)}, u32[]{:S(2)}) copy-start(bf16[1,2560,384]{2,1,0:T(8,128)(2,1)} %get-tuple-element.13) | copy-start | bytes 5898244
  114.7 2.3 %copy-start = (bf16[1,384,2560]{2,1,0:T(8,128)(2,1)S(1)}, bf16[1,384,2560]{2,1,0:T(8,128)(2,1)}, u32[]{:S(2)}) copy-start(bf16[1,384,2560]{2,1,0:T(8,128)(2,1)} %get-tuple-element.14) | copy-start | bytes 5898244

commit v2 on v1

--- a/solution.py
+++ b/solution.py
@@ -47,12 +47,12 @@
 
 
 def kernel(
-    tokens, grad_out, meta_in, wg_hbm, wu_hbm, wd_hbm,
+    tokens, grad_out, routes_hbm, gates_hbm, pull_hbm, counts_hbm, wg_hbm, wu_hbm, wd_hbm,
     mixed, token_grad, gg_hbm, gu_hbm, gd_hbm,
     bx, bdy, sx, sdy, rx, rdy, wg, wu, wd, sel, sel_gate,
     act, slope, hid, gpre, part, out_far, dx_far, out_in, dx_in,
     out_back, dx_back, out_got, dx_got, pout, pdx, zout, zdx, gg, gu, gd,
-    w_sem, z_send, z_recv, x_send, x_recv, c_send, c_recv,
+    routes, gates, pull_list, counts, chosen_t, w_sem, t_sem, z_send, z_recv, y_send, y_recv, x_send, x_recv, c_send, c_recv,
     e_send, e_recv, b_send, b_recv, p_send, p_recv, g_sem,
 ):
     g = lax.axis_index("group")
@@ -75,22 +75,47 @@
 
     sibling = device(x, y, z, 1 - c)
 
-    w_copies = [
-        pltpu.make_async_copy(src.at[0], dst, w_sem.at[i])
-        for i, (src, dst) in enumerate(((wg_hbm, wg), (wu_hbm, wu), (wd_hbm, wd)))
-    ]
-    for copy in w_copies:
-        copy.start()
-
     barrier = pltpu.get_barrier_semaphore()
     near = [z_taker(k) for k in range(1, NZ)] + [z_owner(k) for k in range(1, NZ, 2)]
     near += [device((x + k) % NX, y, z, c) for k in range(1, NX)] + [sibling]
     for other in near:
         pl.semaphore_signal(barrier, inc=1, device_id=other, device_id_type=MESH)
     mine = rows(z, ROWS)
-    bx[mine, :D] = tokens[...]
-    bx[mine, D:] = meta_in[...]
-    bdy[mine, :] = grad_out[...]
+    t_copies = [
+        pltpu.make_async_copy(tokens, bx.at[mine, :D], t_sem.at[0]),
+        pltpu.make_async_copy(grad_out, bdy.at[mine], t_sem.at[1]),
+    ]
+    r_copies = [
+        pltpu.make_async_copy(src, dst, t_sem.at[2 + i])
+        for i, (src, dst) in enumerate(
+            ((routes_hbm, routes), (gates_hbm, gates), (pull_hbm, pull_list), (counts_hbm, counts))
+        )
+    ]
+    w_copies = [
+        pltpu.make_async_copy(src.at[0], dst, w_sem.at[i])
+        for i, (src, dst) in enumerate(((wg_hbm, wg), (wu_hbm, wu), (wd_hbm, wd)))
+    ]
+    for copy in r_copies + t_copies + w_copies:
+        copy.start()
+    for copy in r_copies:
+        copy.wait()
+
+    route = routes[...]
+    expert = g * 16 + route
+    for j in range(8):
+        expert = jnp.where(route == 16 + j, pull_list[g, j], expert)
+    token = d * ROWS + lax.broadcasted_iota(jnp.int32, route.shape, 1)
+    expert = jnp.where(token < counts[g], expert, -1)
+    chosen_t[...] = jnp.zeros_like(chosen_t)
+    chosen_t[:6, :] = expert.astype(F32)
+    chosen_t[8:14, :] = gates[...].astype(F32)
+    k_row = lax.broadcasted_iota(jnp.int32, (ROWS, META), 0)
+    k_lane = lax.broadcasted_iota(jnp.int32, (ROWS, META), 1)
+    spread = (k_lane == k_row) & (k_row < 8) | (k_lane == k_row + (GATE_LANE - 8)) & (k_row >= 8)
+    meta_in = tn(chosen_t[...].astype(BF), jnp.where(spread, 1.0, 0.0).astype(BF))
+    bx[mine, D:] = meta_in.astype(BF)
+    for copy in t_copies:
+        copy.wait()
     pl.semaphore_wait(barrier, len(near))
 
     sent = []
@@ -110,17 +135,67 @@
         ).wait_recv()
 
     far_first = (4, 3, 5, 2, 6, 1, 7)
-    for s, buf in enumerate((bx, bdy)):
-        for k in far_first:
-            send(buf.at[mine], buf.at[mine], z_send.at[s, k], z_recv.at[s, z], z_taker(k))
-
-    def z_arrived(s, buf):
-        for k in range(1, NZ):
-            zz = (z + k) % NZ
-            arrived(buf.at[rows(zz, ROWS)], z_send.at[s, 0], z_recv.at[s, zz])
-
-    z_arrived(0, bx)
-    meta = bx[:, D:].astype(F32)
+    buffers = (bx, bdy)
+    ring = (device(x, y, (z + 1) % NZ, c), device(x, y, (z + NZ - 1) % NZ, c))
+    y_back = device(x, (y + NY - 1) % NY, z, c)
+
+    def slot(block, odd):
+        return rows(jnp.where((odd == 1) & (block % 2 == 0), NZ + block // 2, block), ROWS)
+
+    def lanes_of(s, way, step):
+        width = buffers[s].shape[1]
+        if step < 4:
+            return pl.ds(0, width)
+        return pl.ds(0, D // 2) if way == 0 else pl.ds(D // 2, width - D // 2)
+
+    def ring_block(way, step):
+        return (z + NZ - step) % NZ if way == 0 else (z + step) % NZ
+
+    def pass_on(s, way, step):
+        block, at = ring_block(way, step - 1), lanes_of(s, way, step)
+        send(
+            buffers[s].at[slot(block, z_lo), at], buffers[s].at[slot(block, 1 - z_lo), at],
+            z_send.at[s, way, step], z_recv.at[s, way, step], ring[way],
+        )
+
+    def ring_arrived(s, way, step):
+        at = lanes_of(s, way, step)
+        arrived(
+            buffers[s].at[slot(ring_block(way, step), z_lo), at],
+            z_send.at[s, way, 0], z_recv.at[s, way, step],
+        )
+
+    def y_copy(s, way, step):
+        block = ring_block(way, step)
+        return pltpu.make_async_remote_copy(
+            src_ref=buffers[s].at[slot(block, z_lo)], dst_ref=buffers[s].at[rows(block, ROWS)],
+            send_sem=y_send.at[s, way, step // 2], recv_sem=y_recv.at[s, way, step // 2],
+            device_id=y_back, device_id_type=MESH,
+        )
+
+    def z_arrived(s):
+        for way in range(2):
+            ring_arrived(s, way, 4)
+
+        @pl.when(z_lo == 1)
+        def _():
+            for step in (1, 3):
+                for way in range(2):
+                    y_copy(s, way, step).wait_recv()
+
+    for s in range(2):
+        for way in range(2):
+            pass_on(s, way, 1)
+    for step in (1, 2, 3):
+        for s in range(2):
+            for way in range(2):
+                ring_arrived(s, way, step)
+                pass_on(s, way, step + 1)
+                if step != 2:
+                    pl.when(z_lo == 1)(lambda s=s, way=way, step=step: y_copy(s, way, step).start())
+
+    z_arrived(0)
+    meta = bx[:TOK, D:].astype(F32)
     lane = lax.broadcasted_iota(jnp.int32, (TOK, META), 1)
     gate_at = pltpu.roll(meta, GATE_LANE, 1)
     first = (g * 16 + z_hi * NX).astype(F32)
@@ -155,7 +230,7 @@
 
     def dispatch(s, selector, buf, out, got):
         def body(at):
-            out[:, at] = tn(selector[...], buf[:, at]).astype(BF)
+            out[:, at] = tn(selector[...], buf[:TOK, at]).astype(BF)
 
         over_lanes(body)
         for k in (2, 1, 3):
@@ -177,7 +252,7 @@
             arrived(got.at[rows((1 - c) * NX + j, BLK)], c_send.at[s, 0], c_recv.at[s, j])
 
     dispatch(0, sel, bx, sx, rx)
-    z_arrived(1, bdy)
+    z_arrived(1)
     dispatch(1, sel_gate, bdy, sdy, rdy)
     share(0, rx)
     shared(0, rx)
@@ -275,43 +350,55 @@
     finish(1, zdx, token_grad)
     for copy in sent:
         copy.wait_send()
+
+    @pl.when(z_lo == 1)
+    def _():
+        for s in range(2):
+            for way in range(2):
+                for step in (1, 3):
+                    y_copy(s, way, step).wait_send()
+
     for copy in g_copies:
         copy.wait()
 
 
+def copy_kernel(*refs):
+    n = (len(refs) - 1) // 2
+    sems = refs[-1]
+    copies = []
+    for i in range(n):
+        src, dst = refs[i], refs[n + i]
+        if len(src.shape) == 2:
+            copies.append(pltpu.make_async_copy(src, dst, sems.at[i, 0]))
+            continue
+        part = src.shape[1] // 4
+        for j in range(4):
+            at = pl.ds(j * part, part)
+            copies.append(pltpu.make_async_copy(src.at[0, at], dst.at[0, at], sems.at[i, j]))
+    for copy in copies:
+        copy.start()
+    for copy in copies:
+        copy.wait()
+
+
 def shards(tokens, grad_out, routes, gates, pull_list, counts, w_gate, w_up, w_down):
-    g = lax.axis_index("group")
-    d = lax.axis_index("dev")
-    n_pull = pull_list.shape[1]
-    mine = jnp.arange(pull_list.shape[0]) == g
-    pull_row = jnp.sum(jnp.where(mine[:, None], pull_list, 0), axis=0)
-    count = jnp.sum(jnp.where(mine, counts, 0))
-    pulled = routes[:, :, None] == 16 + jnp.arange(n_pull)[None, None, :]
-    expert = jnp.where(
-        routes < 16, g * 16 + routes, jnp.sum(jnp.where(pulled, pull_row[None, None, :], 0), axis=2)
-    )
-    alive = d * ROWS + jnp.arange(ROWS) < count
-    expert = jnp.where(alive[:, None], expert, -1)
-    gap = jnp.zeros((ROWS, GATE_LANE - routes.shape[1]), BF)
-    meta = jnp.concatenate([expert.astype(BF), gap, gates, gap], axis=1)
-
     vmem = pl.BlockSpec(memory_space=pltpu.VMEM)
     hbm = pl.BlockSpec(memory_space=pl.ANY)
     dma = pltpu.SemaphoreType.DMA
-    return pl.pallas_call(
+    results = pl.pallas_call(
         kernel,
         out_shape=(
-            jax.ShapeDtypeStruct((ROWS, D), BF),
-            jax.ShapeDtypeStruct((ROWS, D), BF),
-            jax.ShapeDtypeStruct((1, D, H), BF),
-            jax.ShapeDtypeStruct((1, D, H), BF),
-            jax.ShapeDtypeStruct((1, H, D), BF),
+            pltpu.VMEM((ROWS, D), BF),
+            pltpu.VMEM((ROWS, D), BF),
+            pltpu.VMEM((1, D, H), BF),
+            pltpu.VMEM((1, D, H), BF),
+            pltpu.VMEM((1, H, D), BF),
         ),
-        in_specs=[vmem] * 3 + [hbm] * 3,
+        in_specs=[pl.BlockSpec(memory_space=pltpu.HBM)] * 9,
         out_specs=(vmem, vmem, hbm, hbm, hbm),
         scratch_shapes=[
-            pltpu.VMEM((TOK, D + META), BF),
-            pltpu.VMEM((TOK, D), BF),
+            pltpu.VMEM((TOK + TOK // 2, D + META), BF),
+            pltpu.VMEM((TOK + TOK // 2, D), BF),
             pltpu.VMEM((HALF, D), BF),
             pltpu.VMEM((HALF, D), BF),
             pltpu.VMEM((ALL, D), BF),
@@ -341,9 +428,17 @@
             pltpu.VMEM((D, H), BF),
             pltpu.VMEM((D, H), BF),
             pltpu.VMEM((H, D), BF),
+            pltpu.VMEM((6, ROWS), jnp.int32),
+            pltpu.VMEM((6, ROWS), BF),
+            pltpu.SMEM((8, 8), jnp.int32),
+            pltpu.SMEM((8,), jnp.int32),
+            pltpu.VMEM((ROWS, ROWS), F32),
             dma((3,)),
-            dma((2, NZ)),
-            dma((2, NZ)),
+            dma((6,)),
+            dma((2, 2, 5)),
+            dma((2, 2, 5)),
+            dma((2, 2, 2)),
+            dma((2, 2, 2)),
             dma((2, NX)),
             dma((2, NX)),
             dma((2, NX)),
@@ -359,7 +454,15 @@
         compiler_params=pltpu.CompilerParams(
             collective_id=0, has_side_effects=True, vmem_limit_bytes=56 * 1024 * 1024
         ),
-    )(tokens, grad_out, meta, w_gate, w_up, w_down)
+    )(tokens, grad_out, routes.T, gates.T, pull_list, counts, w_gate, w_up, w_down)
+    return pl.pallas_call(
+        copy_kernel,
+        out_shape=tuple(jax.ShapeDtypeStruct(r.shape, r.dtype) for r in results),
+        in_specs=[hbm] * 5,
+        out_specs=(hbm,) * 5,
+        scratch_shapes=[dma((5, 4))],
+        compiler_params=pltpu.CompilerParams(vmem_limit_bytes=8 * 1024 * 1024),
+    )(*results)
 
 
 def solution(mesh):

time: 119 us -> 100 us (0.84)
  local copies, waits for them, and re-layouts: 11.4 us -> 0 us
  other arithmetic: 4.25 us -> 0 us
  Pallas kernels: 102 us -> 99.3 us
    unnamed x11 -> x0, local copies, waits for them, and re-layouts: 11.3 us -> none
    reduce_sum x3 -> x0, other arithmetic: 2.84 us -> none  [the longest x1 1.29 us: shards(): count = jnp.sum(jnp.where(mine, counts, 0))]
    pallas_call x1 -> x2, Pallas kernels: 102 us -> 99.3 us  [the longest x1 96.5 us: shards(): pl.pallas_call(kernel, out_shape=(pltpu.VMEM((ROWS, D), BF), pltpu.VMEM((...]
where the time goes in v2:
time: 100 us; the launch traced here: 99.9 us
  Pallas kernels  99.3 us (99%)
    pallas_call x1, Pallas kernels, shards(): pl.pallas_call(kernel, out_shape=(pltpu.VMEM((ROWS, D), BF), pltpu.VMEM((...  96.5 us
    pallas_call x1, Pallas kernels, shards(): pl.pallas_call(copy_kernel, out_shape=tuple((jax.ShapeDtypeStruct(r.shape...  2.76 us

profile of v2, /device:TPU:1, one launch (start us, length us, event | category | flops | bytes accessed | tf_op | source)
XLA Modules:
  0.0 99.9 jit_solution(451740072688023909)
XLA Ops:
  0.6 96.5 %shard_map.128 = (bf16[16,2560]{1,0:T(8,128)(2,1)S(1)}, bf16[16,2560]{1,0:T(8,128)(2,1)S(1)}, bf16[1,2560,384]{2,1,0:T(8,128)(2,1)S(1)}, bf16[1,2560,384]{2,1,0:T(8,128)(2,1)S(1)}, bf16[1,384,2560]{2,1,0:T(8,128)(2,1)S(1)}) custom-call(bf16[16,2560]{1,0:T(8,128)(2,1)} %tokens.1, bf16[16,2560]{1,0:T(8,128)(2,1)} %grad_out.1, s32[6,16]{1,0:T(8,128)} %bitcast.2, ...), custom_call_target="tpu_custom_call" | custom-call | tf_op jit(solution)/shard_map/pallas_call | solution.py:388
  97.1 2.8 %shard_map.129 = (bf16[16,2560]{1,0:T(8,128)(2,1)}, bf16[16,2560]{1,0:T(8,128)(2,1)}, bf16[1,2560,384]{2,1,0:T(8,128)(2,1)}, bf16[1,2560,384]{2,1,0:T(8,128)(2,1)}, bf16[1,384,2560]{2,1,0:T(8,128)(2,1)}) custom-call(bf16[16,2560]{1,0:T(8,128)(2,1)S(1)} %get-tuple-element.10.refs_0_, bf16[16,2560]{1,0:T(8,128)(2,1)S(1)} %get-tuple-element.11.refs_1_, ...), custom_call_target="tpu_custom_call" | custom-call | tf_op jit(solution)/shard_map/pallas_call | solution.py:458

commit v3 on v2

v3 whole, which is shorter than its diff:
```python
import jax
import jax.numpy as jnp
from jax import lax
from jax.experimental import pallas as pl
from jax.experimental.pallas import tpu as pltpu
from jax.sharding import PartitionSpec as P

BF = jnp.bfloat16
F32 = jnp.float32
D = 2560
H = 384
ROWS = 16
CAP = 6
NX, NY, NZ = 4, 4, 8
META = 128
GATE_LANE = 64
BLK = NZ * CAP
HALF = NX * BLK
ALL = 2 * HALF
TOK = NZ * ROWS
HOPS = 4
GATHER = 1280
OUT_W, DX_W = 1280, 640
MESH = pl.DeviceIdType.MESH


def nn(a, b):
    return lax.dot_general(a, b, (((1,), (0,)), ((), ())), preferred_element_type=F32)


def nt(a, b):
    return lax.dot_general(a, b, (((1,), (1,)), ((), ())), preferred_element_type=F32)


def tn(a, b):
    return lax.dot_general(a, b, (((0,), (0,)), ((), ())), preferred_element_type=F32)


def rows(i, n):
    return pl.ds(pl.multiple_of(i * n, n), n)


def kernel(
    tokens, grad_out, routes_hbm, gates_hbm, pull_hbm, counts_hbm, wg_hbm, wu_hbm, wd_hbm,
    mixed, token_grad, gg_hbm, gu_hbm, gd_hbm,
    bm, bx, bdy, sx, sdy, rx, rdy, wg, wu, wd, sel, sel_gate,
    act, slope, hid, gpre, part, far_out, far_dx, near_out, near_dx,
    back_out, back_dx, got_out, got_dx, pout, pdx, via_out, via_dx, end_out, end_dx, gg, gu, gd,
    routes, gates, pull_list, counts, chosen_t, w_sem, t_sem, z_send, z_recv, y_send, y_recv,
    x_send, x_recv, c_send, c_recv, e_send, e_recv, b_send, b_recv, a_send, a_recv, p_send, p_recv, g_sem,
):
    g = lax.axis_index("group")
    d = lax.axis_index("dev")
    y, z_lo = g // 2, g % 2
    z_hi, x, c = d // 8, (d // 2) % 4, d % 2
    z = z_hi * 2 + z_lo

    def device(x_, y_, z_, c_):
        return (y_ * 2 + z_ % 2, ((z_ // 2) * NX + x_) * 2 + c_)

    y_prev = jnp.where(z_lo == 1, y, (y + NY - 1) % NY)
    y_next = jnp.where(z_lo == 0, y, (y + 1) % NY)

    def z_taker(k):
        return device(x, y if k % 2 == 0 else y_prev, (z + k) % NZ, c)

    def z_owner(k):
        return device(x, y if k % 2 == 0 else y_next, (z + k) % NZ, c)

    sibling = device(x, y, z, 1 - c)
    y_back = device(x, (y + NY - 1) % NY, z, c)

    barrier = pltpu.get_barrier_semaphore()
    near = [z_taker(1), z_taker(7), z_owner(1), z_owner(7), z_taker(2), z_taker(6)]
    near += [y_back, device(x, (y + 1) % NY, z, c), sibling]
    near += [device((x + k) % NX, y, z, c) for k in range(1, NX)]
    for other in near:
        pl.semaphore_signal(barrier, inc=1, device_id=other, device_id_type=MESH)
    mine = rows(z, ROWS)
    r_copies = [
        pltpu.make_async_copy(src, dst, t_sem.at[2 + i])
        for i, (src, dst) in enumerate(
            ((routes_hbm, routes), (gates_hbm, gates), (pull_hbm, pull_list), (counts_hbm, counts))
        )
    ]
    t_copies = [
        pltpu.make_async_copy(tokens, bx.at[mine], t_sem.at[0]),
        pltpu.make_async_copy(grad_out, bdy.at[mine], t_sem.at[1]),
    ]
    w_copies = [
        pltpu.make_async_copy(src.at[0], dst, w_sem.at[i])
        for i, (src, dst) in enumerate(((wg_hbm, wg), (wu_hbm, wu), (wd_hbm, wd)))
    ]
    for copy in r_copies + t_copies:
        copy.start()
    for copy in r_copies:
        copy.wait()

    route = routes[...]
    expert = g * 16 + route
    for j in range(8):
        expert = jnp.where(route == 16 + j, pull_list[g, j], expert)
    token = d * ROWS + lax.broadcasted_iota(jnp.int32, route.shape, 1)
    expert = jnp.where(token < counts[g], expert, -1)
    chosen_t[...] = jnp.zeros_like(chosen_t)
    chosen_t[:6, :] = expert.astype(F32)
    chosen_t[8:14, :] = gates[...].astype(F32)
    k_row = lax.broadcasted_iota(jnp.int32, (ROWS, META), 0)
    k_lane = lax.broadcasted_iota(jnp.int32, (ROWS, META), 1)
    spread = (k_lane == k_row) & (k_row < 8) | (k_lane == k_row + (GATE_LANE - 8)) & (k_row >= 8)
    meta_in = tn(chosen_t[...].astype(BF), jnp.where(spread, 1.0, 0.0).astype(BF))
    bm[mine, :] = meta_in.astype(BF)
    for copy in t_copies:
        copy.wait()
    pl.semaphore_wait(barrier, len(near))

    sent = []

    def send(src, dst, s_sem, r_sem, to):
        copy = pltpu.make_async_remote_copy(
            src_ref=src, dst_ref=dst, send_sem=s_sem, recv_sem=r_sem,
            device_id=to, device_id_type=MESH,
        )
        copy.start()
        sent.append(copy)

    def arrived(dst, s_sem, r_sem):
        pltpu.make_async_remote_copy(
            src_ref=dst, dst_ref=dst, send_sem=s_sem, recv_sem=r_sem,
            device_id=sibling, device_id_type=MESH,
        ).wait_recv()

    pieces = [(bm, 0, META)]
    pieces += [(buf, lo, GATHER) for buf in (bx, bdy) for lo in range(0, D, GATHER)]
    n_lo = D // GATHER
    x_pieces, dy_pieces = list(range(1, 1 + n_lo)), list(range(1 + n_lo, 1 + 2 * n_lo))
    ring = (device(x, y, (z + 1) % NZ, c), device(x, y, (z + NZ - 1) % NZ, c))

    def slot(block, odd):
        return rows(jnp.where((odd == 1) & (block % 2 == 0), NZ + block // 2, block), ROWS)

    def ways(i, step):
        return (0,) if i == 0 and step == HOPS else (0, 1)

    def lanes_of(i, way, step):
        buf, lo, width = pieces[i]
        if step < HOPS or i == 0:
            return pl.ds(lo, width)
        return pl.ds(lo + way * (width // 2), width // 2)

    def ring_block(way, step):
        return (z + NZ - step) % NZ if way == 0 else (z + step) % NZ

    def pass_on(i, way, step):
        block, at, buf = ring_block(way, step - 1), lanes_of(i, way, step), pieces[i][0]
        send(
            buf.at[slot(block, z_lo), at], buf.at[slot(block, 1 - z_lo), at],
            z_send.at[i, way, step], z_recv.at[i, way, step], ring[way],
        )

    def ring_arrived(i, way, step):
        at = lanes_of(i, way, step)
        arrived(pieces[i][0].at[slot(ring_block(way, step), z_lo), at], z_send.at[i, way, 0], z_recv.at[i, way, step])

    def y_copy(i, way, step):
        block, at, buf = ring_block(way, step), lanes_of(i, way, 1), pieces[i][0]
        return pltpu.make_async_remote_copy(
            src_ref=buf.at[slot(block, z_lo), at], dst_ref=buf.at[rows(block, ROWS), at],
            send_sem=y_send.at[i, way, step // 2], recv_sem=y_recv.at[i, way, step // 2],
            device_id=y_back, device_id_type=MESH,
        )

    def start(i):
        for way in range(2):
            pass_on(i, way, 1)

    def relay(i, step):
        for way in range(2):
            ring_arrived(i, way, step)
            if way in ways(i, step + 1):
                pass_on(i, way, step + 1)
            if step != 2:
                pl.when(z_lo == 1)(lambda: y_copy(i, way, step).start())

    def gathered(i):
        for way in ways(i, HOPS):
            ring_arrived(i, way, HOPS)

        @pl.when(z_lo == 1)
        def _():
            for step in (1, 3):
                for way in range(2):
                    y_copy(i, way, step).wait_recv()

    start(0)
    for i in x_pieces:
        start(i)
    for copy in w_copies:
        copy.start()
    for i in [0] + x_pieces:
        relay(i, 1)
    for i in dy_pieces:
        start(i)
    for i in [0] + x_pieces:
        relay(i, 2)
    for i in dy_pieces:
        relay(i, 1)
    for i in [0] + x_pieces:
        relay(i, 3)
    for i in dy_pieces:
        relay(i, 2)

    gathered(0)
    meta = bm[:TOK, :].astype(F32)
    lane = lax.broadcasted_iota(jnp.int32, (TOK, META), 1)
    gate_at = pltpu.roll(meta, GATE_LANE, 1)
    first = (g * 16 + z_hi * NX).astype(F32)
    hits, gate_of = [], []
    hit_all = jnp.zeros((TOK, META), F32)
    for j in range(NX):
        match = jnp.where((meta == first + j) & (lane < 6), 1.0, 0.0)
        hits.append(jnp.sum(match, axis=1, keepdims=True))
        gate_of.append(jnp.sum(match * gate_at, axis=1, keepdims=True))
        hit_all = hit_all + jnp.where(lane == j, hits[j], 0.0)
    t_row = lax.broadcasted_iota(jnp.int32, (TOK, TOK), 0)
    t_col = lax.broadcasted_iota(jnp.int32, (TOK, TOK), 1)
    before = jnp.where((t_col < t_row) & (t_col // ROWS == t_row // ROWS), 1.0, 0.0)
    rank_all = nn(before.astype(BF), hit_all.astype(BF))
    q = lax.broadcasted_iota(jnp.int32, (TOK, HALF), 1)
    block = lax.broadcasted_iota(jnp.int32, (TOK, HALF), 0) // ROWS
    place = jnp.zeros((TOK, HALF), F32)
    hit_q = jnp.zeros((TOK, HALF), F32)
    gate_q = jnp.zeros((TOK, HALF), F32)
    for j in range(NX):
        rank = jnp.sum(jnp.where(lane == j, rank_all, 0.0), axis=1, keepdims=True)
        inside = (q >= j * BLK) & (q < (j + 1) * BLK)
        place = jnp.where(inside, rank + j * BLK, place)
        hit_q = jnp.where(inside, hits[j], hit_q)
        gate_q = jnp.where(inside, gate_of[j], gate_q)
    placed = place + (block * CAP).astype(F32) == q.astype(F32)
    chosen = jnp.where(placed, hit_q, 0.0)
    sel[...] = chosen.astype(BF)
    sel_gate[...] = (chosen * gate_q).astype(BF)

    my_slot = rows(c * NX + x, BLK)
    dests = {i: (sx, rx) for i in x_pieces} | {i: (sdy, rdy) for i in dy_pieces}

    def dispatch(i, selector):
        buf, lo, width = pieces[i]
        out, got = dests[i]
        at = pl.ds(lo, width)
        gathered(i)
        out[:, at] = tn(selector[...], buf[:TOK, at]).astype(BF)
        for k in (2, 1, 3):
            j = (x + k) % NX
            send(out.at[rows(j, BLK), at], got.at[my_slot, at], x_send.at[i, k], x_recv.at[i, x], device(j, y, z, c))
        got[my_slot, at] = out[rows(x, BLK), at]
        send(got.at[my_slot, at], got.at[my_slot, at], c_send.at[i, 0], c_recv.at[i, x], sibling)

    def share(i):
        at, got = pl.ds(pieces[i][1], GATHER), dests[i][1]
        for k in (1, 3, 2):
            j = (x + k) % NX
            here = got.at[rows(c * NX + j, BLK), at]
            arrived(here, x_send.at[i, 0], x_recv.at[i, j])
            send(here, here, c_send.at[i, k], c_recv.at[i, j], sibling)

    def shared(i):
        at, got = pl.ds(pieces[i][1], GATHER), dests[i][1]
        for k in range(NX):
            j = (x + k) % NX
            arrived(got.at[rows((1 - c) * NX + j, BLK), at], c_send.at[i, 0], c_recv.at[i, j])

    for i in x_pieces[:1]:
        dispatch(i, sel)
    for i in dy_pieces:
        relay(i, 3)
    for i in x_pieces[1:]:
        dispatch(i, sel)
    for i in dy_pieces:
        dispatch(i, sel_gate)

    for copy in w_copies:
        copy.wait()
    pre_gate, pre_up = act, slope
    for n, i in enumerate(x_pieces):
        share(i)
        shared(i)
        at = pl.ds(pieces[i][1], GATHER)
        by_gate, by_up = nn(rx[:, at], wg[at, :]), nn(rx[:, at], wu[at, :])
        pre_gate[...] = by_gate if n == 0 else pre_gate[...] + by_gate
        pre_up[...] = by_up if n == 0 else pre_up[...] + by_up
    v_gate, v_up = pre_gate[...], pre_up[...]
    sig = jax.nn.sigmoid(v_gate)
    silu = v_gate * sig
    hid[...] = (silu * v_up).astype(BF)
    act[...] = silu
    slope[...] = v_up * sig * (1.0 + v_gate * (1.0 - sig))

    far_rows, own_rows = rows(1 - c, HALF), rows(c, HALF)
    back_pieces = [(0, lo, OUT_W) for lo in range(0, D, OUT_W)] + [(1, lo, DX_W) for lo in range(0, D, DX_W)]
    n_out = D // OUT_W
    out_back, dx_back = list(range(n_out)), list(range(n_out, len(back_pieces)))
    buffers = (
        (far_out, near_out, back_out, got_out, pout, via_out, end_out),
        (far_dx, near_dx, back_dx, got_dx, pdx, via_dx, end_dx),
    )

    def rows_of(s, r, at):
        if s == 0:
            return nn(hid[r, :], wd[:, at])
        return nt(gpre[r, :H], wg[at, :]) + nt(gpre[r, H:], wu[at, :])

    def back(todo):
        for i in todo:
            s, lo, width = back_pieces[i]
            far, near_in = buffers[s][:2]
            at = pl.ds(lo, width)
            far[:, at] = rows_of(s, far_rows, at).astype(BF)
            send(far.at[:, at], near_in.at[:, at], e_send.at[i], e_recv.at[i], sibling)
        for i in todo:
            s, lo, width = back_pieces[i]
            at = pl.ds(lo, width)
            part[:, at] = rows_of(s, own_rows, at)

    def give_back(i):
        s, lo, width = back_pieces[i]
        _, near_in, summed, got = buffers[s][:4]
        at = pl.ds(lo, width)
        arrived(near_in.at[:, at], e_send.at[i], e_recv.at[i])
        summed[:, at] = (part[:, at] + near_in[:, at].astype(F32)).astype(BF)
        for k in (2, 1, 3):
            j = (x + k) % NX
            send(
                summed.at[rows(j, BLK), at], got.at[rows(x, BLK), at],
                b_send.at[i, k], b_recv.at[i, x], device(j, y, z, c),
            )
        got[rows(x, BLK), at] = summed[rows(x, BLK), at]

    def split(i, way):
        lo, width = back_pieces[i][1:]
        first_part = (width // 2 + 127) // 128 * 128
        return pl.ds(lo, first_part) if way == 0 else pl.ds(lo + first_part, width - first_part)

    def combine(i, selector):
        s, lo, width = back_pieces[i]
        got, partial, via = buffers[s][3:6]
        at = pl.ds(lo, width)
        for k in range(1, NX):
            j = (x + k) % NX
            arrived(got.at[rows(j, BLK), at], b_send.at[i, 0], b_recv.at[i, j])
        partial[:, at] = nn(selector[...], got[:, at]).astype(BF)
        middle = rows((z + 4) % NZ, ROWS)
        for way, k in ((0, 3), (1, 5)):
            to = z_owner(2 if way == 0 else 6)
            outer = rows((z + k) % NZ, ROWS)
            send(partial.at[outer, at], via.at[rows(way, ROWS), at], a_send.at[i, way, 0], a_recv.at[i, way, 0], to)
            half = split(i, way)
            send(partial.at[middle, half], via.at[rows(2 + way, ROWS), half], a_send.at[i, way, 1], a_recv.at[i, way, 1], to)

    def send_home(i):
        s, lo, width = back_pieces[i]
        partial, via, end = buffers[s][4:]
        at = pl.ds(lo, width)
        for way, k in ((0, 1), (1, 7)):
            outer, half = rows(way, ROWS), split(i, way)
            arrived(via.at[outer, at], a_send.at[i, way, 0], a_recv.at[i, way, 0])
            spot = rows((z + k) % NZ, ROWS)
            partial[spot, at] = (partial[spot, at].astype(F32) + via[outer, at].astype(F32)).astype(BF)
            send(partial.at[spot, at], end.at[rows(way, ROWS), at], p_send.at[i, way, 0], p_recv.at[i, way, 0], z_owner(k))
            inner = rows(2 + way, ROWS)
            arrived(via.at[inner, half], a_send.at[i, way, 1], a_recv.at[i, way, 1])
            spot = rows((z + 2 * k) % NZ, ROWS)
            partial[spot, half] = (partial[spot, half].astype(F32) + via[inner, half].astype(F32)).astype(BF)
            send(partial.at[spot, at], end.at[inner, at], p_send.at[i, way, 1], p_recv.at[i, way, 1], z_owner((2 * k) % NZ))

    def finish(i, result):
        s, lo, width = back_pieces[i]
        partial, _, end = buffers[s][4:]
        at = pl.ds(lo, width)
        total = partial[mine, at].astype(F32)
        for n in range(2):
            for way in range(2):
                there = rows(2 * n + way, ROWS)
                arrived(end.at[there, at], p_send.at[i, way, n], p_recv.at[i, way, n])
                total = total + end[there, at].astype(F32)
        result[:, at] = total.astype(BF)

    back(out_back)
    for i in out_back:
        give_back(i)
    back_hidden = jnp.zeros((ALL, H), F32)
    for i in dy_pieces:
        share(i)
        shared(i)
        at = pl.ds(pieces[i][1], GATHER)
        back_hidden = back_hidden + nt(rdy[:, at], wd[:, at])
    gpre[:, :H] = (back_hidden * slope[...]).astype(BF)
    gpre[:, H:] = (back_hidden * act[...]).astype(BF)
    back(dx_back)
    for i in dx_back:
        give_back(i)
    combine(out_back[0], sel_gate)

    for lo in range(0, D, 1280):
        at = pl.ds(lo, 1280)
        both = tn(rx[:, at], gpre[...])
        gg[at, :] = both[:, :H].astype(BF)
        gu[at, :] = both[:, H:].astype(BF)
        gd[:, at] = tn(hid[...], rdy[:, at]).astype(BF)
    g_copies = [
        pltpu.make_async_copy(src, dst.at[0], g_sem.at[i])
        for i, (src, dst) in enumerate(((gg, gg_hbm), (gu, gu_hbm), (gd, gd_hbm)))
    ]
    for copy in g_copies:
        copy.start()

    todo = [(i, sel_gate) for i in out_back[1:]] + [(i, sel) for i in dx_back]
    last = out_back[0]
    for i, selector in todo:
        combine(i, selector)
        send_home(last)
        last = i
    send_home(last)
    for i in out_back:
        finish(i, mixed)
    for i in dx_back:
        finish(i, token_grad)
    for copy in sent:
        copy.wait_send()

    @pl.when(z_lo == 1)
    def _():
        for i in range(len(pieces)):
            for way in range(2):
                for step in (1, 3):
                    y_copy(i, way, step).wait_send()

    for copy in g_copies:
        copy.wait()


def copy_kernel(*refs):
    n = (len(refs) - 1) // 2
    sems = refs[-1]
    copies = []
    for i in range(n):
        src, dst = refs[i], refs[n + i]
        if len(src.shape) == 2:
            copies.append(pltpu.make_async_copy(src, dst, sems.at[i, 0]))
            continue
        part = src.shape[1] // 4
        for j in range(4):
            at = pl.ds(j * part, part)
            copies.append(pltpu.make_async_copy(src.at[0, at], dst.at[0, at], sems.at[i, j]))
    for copy in copies:
        copy.start()
    for copy in copies:
        copy.wait()


def shards(tokens, grad_out, routes, gates, pull_list, counts, w_gate, w_up, w_down):
    vmem = pl.BlockSpec(memory_space=pltpu.VMEM)
    hbm = pl.BlockSpec(memory_space=pl.ANY)
    dma = pltpu.SemaphoreType.DMA
    n_gather = 1 + 2 * (D // GATHER)
    n_back = D // OUT_W + D // DX_W
    results = pl.pallas_call(
        kernel,
        out_shape=(
            pltpu.VMEM((ROWS, D), BF),
            pltpu.VMEM((ROWS, D), BF),
            pltpu.VMEM((1, D, H), BF),
            pltpu.VMEM((1, D, H), BF),
            pltpu.VMEM((1, H, D), BF),
        ),
        in_specs=[pl.BlockSpec(memory_space=pltpu.HBM)] * 9,
        out_specs=(vmem, vmem, hbm, hbm, hbm),
        scratch_shapes=[
            pltpu.VMEM((TOK + TOK // 2, META), BF),
            pltpu.VMEM((TOK + TOK // 2, D), BF),
            pltpu.VMEM((TOK + TOK // 2, D), BF),
            pltpu.VMEM((HALF, D), BF),
            pltpu.VMEM((HALF, D), BF),
            pltpu.VMEM((ALL, D), BF),
            pltpu.VMEM((ALL, D), BF),
            pltpu.VMEM((D, H), BF),
            pltpu.VMEM((D, H), BF),
            pltpu.VMEM((H, D), BF),
            pltpu.VMEM((TOK, HALF), BF),
            pltpu.VMEM((TOK, HALF), BF),
            pltpu.VMEM((ALL, H), F32),
            pltpu.VMEM((ALL, H), F32),
            pltpu.VMEM((ALL, H), BF),
            pltpu.VMEM((ALL, 2 * H), BF),
            pltpu.VMEM((HALF, D), F32),
            pltpu.VMEM((HALF, D), BF),
            pltpu.VMEM((HALF, D), BF),
            pltpu.VMEM((HALF, D), BF),
            pltpu.VMEM((HALF, D), BF),
            pltpu.VMEM((HALF, D), BF),
            pltpu.VMEM((HALF, D), BF),
            pltpu.VMEM((HALF, D), BF),
            pltpu.VMEM((HALF, D), BF),
            pltpu.VMEM((TOK, D), BF),
            pltpu.VMEM((TOK, D), BF),
            pltpu.VMEM((4 * ROWS, D), BF),
            pltpu.VMEM((4 * ROWS, D), BF),
            pltpu.VMEM((4 * ROWS, D), BF),
            pltpu.VMEM((4 * ROWS, D), BF),
            pltpu.VMEM((D, H), BF),
            pltpu.VMEM((D, H), BF),
            pltpu.VMEM((H, D), BF),
            pltpu.VMEM((6, ROWS), jnp.int32),
            pltpu.VMEM((6, ROWS), BF),
            pltpu.SMEM((8, 8), jnp.int32),
            pltpu.SMEM((8,), jnp.int32),
            pltpu.VMEM((ROWS, ROWS), F32),
            dma((3,)),
            dma((6,)),
            dma((n_gather, 2, HOPS + 1)),
            dma((n_gather, 2, HOPS + 1)),
            dma((n_gather, 2, 2)),
            dma((n_gather, 2, 2)),
            dma((n_gather, NX)),
            dma((n_gather, NX)),
            dma((n_gather, NX)),
            dma((n_gather, NX)),
            dma((n_back,)),
            dma((n_back,)),
            dma((n_back, NX)),
            dma((n_back, NX)),
            dma((n_back, 2, 2)),
            dma((n_back, 2, 2)),
            dma((n_back, 2, 2)),
            dma((n_back, 2, 2)),
            dma((3,)),
        ],
        compiler_params=pltpu.CompilerParams(
            collective_id=0, has_side_effects=True, vmem_limit_bytes=56 * 1024 * 1024
        ),
    )(tokens, grad_out, routes.T, gates.T, pull_list, counts, w_gate, w_up, w_down)
    return pl.pallas_call(
        copy_kernel,
        out_shape=tuple(jax.ShapeDtypeStruct(r.shape, r.dtype) for r in results),
        in_specs=[hbm] * 5,
        out_specs=(hbm,) * 5,
        scratch_shapes=[dma((5, 4))],
        compiler_params=pltpu.CompilerParams(vmem_limit_bytes=8 * 1024 * 1024),
    )(*results)


def solution(mesh):
    both = ("group", "dev")
    in_specs = (
        P(both, None), P(both, None), P(both, None), P(both, None), P(), P(),
        P(both, None, None), P(both, None, None), P(both, None, None),
    )
    out_specs = (
        P(both, None), P(both, None),
        P(both, None, None), P(both, None, None), P(both, None, None),
    )
    return jax.shard_map(shards, mesh=mesh, in_specs=in_specs, out_specs=out_specs, check_vma=False)
```

time: 100 us -> 87.2 us (0.87)
  Pallas kernels: 99.3 us -> 86.4 us
    pallas_call x1, Pallas kernels: 96.5 us -> 83.6 us  [shards(): pl.pallas_call(kernel, out_shape=(pltpu.VMEM((ROWS, D), BF), pltpu.VMEM((...]
where the time goes in v3:
time: 87.2 us; the launch traced here: 87 us
  Pallas kernels  86.4 us (99%)
    pallas_call x1, Pallas kernels, shards(): pl.pallas_call(kernel, out_shape=(pltpu.VMEM((ROWS, D), BF), pltpu.VMEM((...  83.6 us
    pallas_call x1, Pallas kernels, shards(): pl.pallas_call(copy_kernel, out_shape=tuple((jax.ShapeDtypeStruct(r.shape...  2.76 us

profile of v3, /device:TPU:1, one launch (start us, length us, event | category | flops | bytes accessed | tf_op | source)
XLA Modules:
  0.0 87.0 jit_solution(9067035390496584446)
XLA Ops:
  0.6 83.6 %shard_map.128 = (bf16[16,2560]{1,0:T(8,128)(2,1)S(1)}, bf16[16,2560]{1,0:T(8,128)(2,1)S(1)}, bf16[1,2560,384]{2,1,0:T(8,128)(2,1)S(1)}, bf16[1,2560,384]{2,1,0:T(8,128)(2,1)S(1)}, bf16[1,384,2560]{2,1,0:T(8,128)(2,1)S(1)}) custom-call(bf16[16,2560]{1,0:T(8,128)(2,1)} %tokens.1, bf16[16,2560]{1,0:T(8,128)(2,1)} %grad_out.1, s32[6,16]{1,0:T(8,128)} %bitcast.2, ...), custom_call_target="tpu_custom_call" | custom-call | tf_op jit(solution)/shard_map/pallas_call | solution.py:468
  84.3 2.8 %shard_map.129 = (bf16[16,2560]{1,0:T(8,128)(2,1)}, bf16[16,2560]{1,0:T(8,128)(2,1)}, bf16[1,2560,384]{2,1,0:T(8,128)(2,1)}, bf16[1,2560,384]{2,1,0:T(8,128)(2,1)}, bf16[1,384,2560]{2,1,0:T(8,128)(2,1)}) custom-call(bf16[16,2560]{1,0:T(8,128)(2,1)S(1)} %get-tuple-element.10.refs_0_, bf16[16,2560]{1,0:T(8,128)(2,1)S(1)} %get-tuple-element.11.refs_1_, ...), custom_call_target="tpu_custom_call" | custom-call | tf_op jit(solution)/shard_map/pallas_call | solution.py:543

commit v4 on v3

--- a/solution.py
+++ b/solution.py
@@ -19,9 +19,16 @@
 ALL = 2 * HALF
 TOK = NZ * ROWS
 HOPS = 4
-GATHER = 1280
-OUT_W, DX_W = 1280, 640
+X_CUT, DY_CUT = (1280, 1280), (1280, 1280)
+OUT_CUT, DX_CUT = (1280, 1280), (1280, 1280)
+ORDER = (0, 1, 7, 2, 6, 3, 5, 4)
+EARLY = 16
 MESH = pl.DeviceIdType.MESH
+
+
+def cut(widths):
+    starts = [sum(widths[:n]) for n in range(len(widths))]
+    return list(zip(starts, widths))
 
 
 def nn(a, b):
@@ -131,66 +138,168 @@
         ).wait_recv()
 
     pieces = [(bm, 0, META)]
-    pieces += [(buf, lo, GATHER) for buf in (bx, bdy) for lo in range(0, D, GATHER)]
-    n_lo = D // GATHER
-    x_pieces, dy_pieces = list(range(1, 1 + n_lo)), list(range(1 + n_lo, 1 + 2 * n_lo))
+    pieces += [(bx, lo, width) for lo, width in cut(X_CUT)] + [(bdy, lo, width) for lo, width in cut(DY_CUT)]
+    x_pieces = list(range(1, 1 + len(X_CUT)))
+    dy_pieces = list(range(1 + len(X_CUT), len(pieces)))
     ring = (device(x, y, (z + 1) % NZ, c), device(x, y, (z + NZ - 1) % NZ, c))
+    skip = (device(x, y, (z + 2) % NZ, c), device(x, y, (z + NZ - 2) % NZ, c))
 
     def slot(block, odd):
         return rows(jnp.where((odd == 1) & (block % 2 == 0), NZ + block // 2, block), ROWS)
 
-    def ways(i, step):
-        return (0,) if i == 0 and step == HOPS else (0, 1)
-
-    def lanes_of(i, way, step):
-        buf, lo, width = pieces[i]
-        if step < HOPS or i == 0:
-            return pl.ds(lo, width)
-        return pl.ds(lo + way * (width // 2), width // 2)
-
     def ring_block(way, step):
         return (z + NZ - step) % NZ if way == 0 else (z + step) % NZ
 
-    def pass_on(i, way, step):
-        block, at, buf = ring_block(way, step - 1), lanes_of(i, way, step), pieces[i][0]
+    def by_core(first, second):
+        return jnp.where(c == 0, first, second)
+
+    def pass_on(i, way, block, step):
+        buf, lo, width = pieces[i]
+        at = pl.ds(lo, width)
         send(
             buf.at[slot(block, z_lo), at], buf.at[slot(block, 1 - z_lo), at],
             z_send.at[i, way, step], z_recv.at[i, way, step], ring[way],
         )
 
+    def pass_last(i):
+        buf, lo, width = pieces[i]
+        at = pl.ds(lo, width)
+        block = by_core(ring_block(0, 3), ring_block(1, 3))
+        there = by_core((z + 1) % NZ, (z + NZ - 1) % NZ)
+        send(
+            buf.at[slot(block, z_lo), at], buf.at[slot(block, 1 - z_lo), at],
+            z_send.at[i, 0, HOPS], z_recv.at[i, 0, HOPS], device(x, y, there, c),
+        )
+
     def ring_arrived(i, way, step):
-        at = lanes_of(i, way, step)
-        arrived(pieces[i][0].at[slot(ring_block(way, step), z_lo), at], z_send.at[i, way, 0], z_recv.at[i, way, step])
+        buf, lo, width = pieces[i]
+        arrived(buf.at[slot(ring_block(way, step), z_lo), pl.ds(lo, width)], z_send.at[i, way, 0], z_recv.at[i, way, step])
 
     def y_copy(i, way, step):
-        block, at, buf = ring_block(way, step), lanes_of(i, way, 1), pieces[i][0]
+        buf, lo, width = pieces[i]
+        block, at = ring_block(way, step), pl.ds(lo, width)
         return pltpu.make_async_remote_copy(
             src_ref=buf.at[slot(block, z_lo), at], dst_ref=buf.at[rows(block, ROWS), at],
             send_sem=y_send.at[i, way, step // 2], recv_sem=y_recv.at[i, way, step // 2],
             device_id=y_back, device_id_type=MESH,
         )
 
+    def y_arrived(i, step):
+        @pl.when(z_lo == 1)
+        def _():
+            for way in range(2):
+                y_copy(i, way, step).wait_recv()
+
     def start(i):
         for way in range(2):
-            pass_on(i, way, 1)
+            pass_on(i, way, z, 1)
 
     def relay(i, step):
         for way in range(2):
             ring_arrived(i, way, step)
-            if way in ways(i, step + 1):
-                pass_on(i, way, step + 1)
+            if step < 3:
+                pass_on(i, way, ring_block(way, step), step + 1)
             if step != 2:
                 pl.when(z_lo == 1)(lambda: y_copy(i, way, step).start())
+        if step == 3:
+            pass_last(i)
 
     def gathered(i):
-        for way in ways(i, HOPS):
-            ring_arrived(i, way, HOPS)
-
-        @pl.when(z_lo == 1)
-        def _():
-            for step in (1, 3):
-                for way in range(2):
-                    y_copy(i, way, step).wait_recv()
+        ring_arrived(i, 0, HOPS)
+        y_arrived(i, 3)
+
+    def ordered(buf, lo, hi, at):
+        return jnp.concatenate([buf[rows((z + ORDER[n]) % NZ, ROWS), at] for n in range(lo, hi)], axis=0)
+
+    def choices(lo, hi):
+        meta = ordered(bm, lo, hi, slice(None)).astype(F32)
+        n = meta.shape[0]
+        lane = lax.broadcasted_iota(jnp.int32, (n, META), 1)
+        gate_at = pltpu.roll(meta, GATE_LANE, 1)
+        first = (g * 16 + z_hi * NX).astype(F32)
+        hits, gate_of = [], []
+        hit_all = jnp.zeros((n, META), F32)
+        for j in range(NX):
+            match = jnp.where((meta == first + j) & (lane < 6), 1.0, 0.0)
+            hits.append(jnp.sum(match, axis=1, keepdims=True))
+            gate_of.append(jnp.sum(match * gate_at, axis=1, keepdims=True))
+            hit_all = hit_all + jnp.where(lane == j, hits[j], 0.0)
+        t_row = lax.broadcasted_iota(jnp.int32, (n, n), 0)
+        t_col = lax.broadcasted_iota(jnp.int32, (n, n), 1)
+        before = jnp.where((t_col < t_row) & (t_col // ROWS == t_row // ROWS), 1.0, 0.0)
+        rank_all = nn(before.astype(BF), hit_all.astype(BF))
+        ranks = [jnp.sum(jnp.where(lane == j, rank_all, 0.0), axis=1, keepdims=True) for j in range(NX)]
+        return hits, gate_of, ranks
+
+    def selectors(chosen, lo, first, count):
+        hits, gate_of, ranks = chosen
+        n = hits[0].shape[0]
+        q = lax.broadcasted_iota(jnp.int32, (n, NX * count), 1)
+        block = lax.broadcasted_iota(jnp.int32, (n, NX * count), 0) // ROWS + lo
+        place = jnp.zeros((n, NX * count), F32)
+        hit_q = jnp.zeros((n, NX * count), F32)
+        gate_q = jnp.zeros((n, NX * count), F32)
+        start_q = jnp.zeros((n, NX * count), jnp.int32)
+        for j in range(NX):
+            inside = (q >= j * count) & (q < (j + 1) * count)
+            start_q = jnp.where(inside, j * count, start_q)
+            place = jnp.where(inside, ranks[j], place)
+            hit_q = jnp.where(inside, hits[j], hit_q)
+            gate_q = jnp.where(inside, gate_of[j], gate_q)
+        placed = place + (block * CAP).astype(F32) == (q - start_q + first).astype(F32)
+        picked = jnp.where(placed, hit_q, 0.0)
+        return picked.astype(BF), (picked * gate_q).astype(BF)
+
+    my_slot = rows(c * NX + x, BLK)
+    dests = {i: (sx, rx) for i in x_pieces} | {i: (sdy, rdy) for i in dy_pieces}
+    first_of = {x_pieces[0]: 0, dy_pieces[0]: len(pieces)}
+
+    def hand_out(out, got, at, lo, count, n):
+        here = pl.ds(pl.multiple_of((c * NX + x) * BLK + lo, 16), count)
+        for k in (2, 1, 3):
+            j = (x + k) % NX
+            there = pl.ds(pl.multiple_of(j * BLK + lo, 16), count)
+            send(out.at[there, at], got.at[here, at], x_send.at[n, k], x_recv.at[n, x], device(j, y, z, c))
+        got[here, at] = out[pl.ds(pl.multiple_of(x * BLK + lo, 16), count), at]
+
+    def dispatch_early(todo, selector):
+        for i in todo:
+            y_arrived(i, 1)
+        buf, (out, got) = pieces[todo[0]][0], dests[todo[0]]
+        picked = tn(selector, ordered(buf, 0, 3, slice(None))).astype(BF)
+        for j in range(NX):
+            out[j * BLK:j * BLK + EARLY, :] = picked[j * EARLY:(j + 1) * EARLY, :]
+        hand_out(out, got, pl.ds(0, D), 0, EARLY, first_of[todo[0]])
+
+    def dispatch(i, selector):
+        buf, lo, width = pieces[i]
+        out, got = dests[i]
+        at = pl.ds(lo, width)
+        gathered(i)
+        picked = tn(selector, ordered(buf, 2, NZ, at)).astype(BF)
+        late = BLK - EARLY
+        for j in range(NX):
+            out[j * BLK + EARLY:(j + 1) * BLK, at] = picked[j * late:(j + 1) * late, :]
+        hand_out(out, got, at, EARLY, late, i)
+        send(got.at[my_slot, at], got.at[my_slot, at], c_send.at[i, 0], c_recv.at[i, x], sibling)
+
+    def share(i):
+        at, got = pl.ds(*pieces[i][1:]), dests[i][1]
+        for k in (1, 3, 2):
+            j = (x + k) % NX
+            here = got.at[rows(c * NX + j, BLK), at]
+            if i in first_of:
+                n, early_rows = first_of[i], pl.ds(pl.multiple_of((c * NX + j) * BLK, 16), EARLY)
+                arrived(got.at[early_rows], x_send.at[n, 0], x_recv.at[n, j])
+            late_rows = pl.ds(pl.multiple_of((c * NX + j) * BLK + EARLY, 16), BLK - EARLY)
+            arrived(got.at[late_rows, at], x_send.at[i, 0], x_recv.at[i, j])
+            send(here, here, c_send.at[i, k], c_recv.at[i, j], sibling)
+
+    def shared(i):
+        at, got = pl.ds(*pieces[i][1:]), dests[i][1]
+        for k in range(NX):
+            j = (x + k) % NX
+            arrived(got.at[rows((1 - c) * NX + j, BLK), at], c_send.at[i, 0], c_recv.at[i, j])
 
     start(0)
     for i in x_pieces:
@@ -199,86 +308,31 @@
         copy.start()
     for i in [0] + x_pieces:
         relay(i, 1)
-    for i in dy_pieces:
-        start(i)
     for i in [0] + x_pieces:
         relay(i, 2)
     for i in dy_pieces:
-        relay(i, 1)
+        start(i)
+    y_arrived(0, 1)
+    early_sel, early_gate = selectors(choices(0, 3), 0, 0, EARLY)
+    dispatch_early(x_pieces, early_sel)
     for i in [0] + x_pieces:
         relay(i, 3)
     for i in dy_pieces:
+        relay(i, 1)
+    gathered(0)
+    chosen = choices(0, NZ)
+    late_sel, late_gate = selectors([[v[2 * ROWS:] for v in vs] for vs in chosen], 2, EARLY, BLK - EARLY)
+    dispatch(x_pieces[0], late_sel)
+    for i in dy_pieces:
         relay(i, 2)
-
-    gathered(0)
-    meta = bm[:TOK, :].astype(F32)
-    lane = lax.broadcasted_iota(jnp.int32, (TOK, META), 1)
-    gate_at = pltpu.roll(meta, GATE_LANE, 1)
-    first = (g * 16 + z_hi * NX).astype(F32)
-    hits, gate_of = [], []
-    hit_all = jnp.zeros((TOK, META), F32)
-    for j in range(NX):
-        match = jnp.where((meta == first + j) & (lane < 6), 1.0, 0.0)
-        hits.append(jnp.sum(match, axis=1, keepdims=True))
-        gate_of.append(jnp.sum(match * gate_at, axis=1, keepdims=True))
-        hit_all = hit_all + jnp.where(lane == j, hits[j], 0.0)
-    t_row = lax.broadcasted_iota(jnp.int32, (TOK, TOK), 0)
-    t_col = lax.broadcasted_iota(jnp.int32, (TOK, TOK), 1)
-    before = jnp.where((t_col < t_row) & (t_col // ROWS == t_row // ROWS), 1.0, 0.0)
-    rank_all = nn(before.astype(BF), hit_all.astype(BF))
-    q = lax.broadcasted_iota(jnp.int32, (TOK, HALF), 1)
-    block = lax.broadcasted_iota(jnp.int32, (TOK, HALF), 0) // ROWS
-    place = jnp.zeros((TOK, HALF), F32)
-    hit_q = jnp.zeros((TOK, HALF), F32)
-    gate_q = jnp.zeros((TOK, HALF), F32)
-    for j in range(NX):
-        rank = jnp.sum(jnp.where(lane == j, rank_all, 0.0), axis=1, keepdims=True)
-        inside = (q >= j * BLK) & (q < (j + 1) * BLK)
-        place = jnp.where(inside, rank + j * BLK, place)
-        hit_q = jnp.where(inside, hits[j], hit_q)
-        gate_q = jnp.where(inside, gate_of[j], gate_q)
-    placed = place + (block * CAP).astype(F32) == q.astype(F32)
-    chosen = jnp.where(placed, hit_q, 0.0)
-    sel[...] = chosen.astype(BF)
-    sel_gate[...] = (chosen * gate_q).astype(BF)
-
-    my_slot = rows(c * NX + x, BLK)
-    dests = {i: (sx, rx) for i in x_pieces} | {i: (sdy, rdy) for i in dy_pieces}
-
-    def dispatch(i, selector):
-        buf, lo, width = pieces[i]
-        out, got = dests[i]
-        at = pl.ds(lo, width)
-        gathered(i)
-        out[:, at] = tn(selector[...], buf[:TOK, at]).astype(BF)
-        for k in (2, 1, 3):
-            j = (x + k) % NX
-            send(out.at[rows(j, BLK), at], got.at[my_slot, at], x_send.at[i, k], x_recv.at[i, x], device(j, y, z, c))
-        got[my_slot, at] = out[rows(x, BLK), at]
-        send(got.at[my_slot, at], got.at[my_slot, at], c_send.at[i, 0], c_recv.at[i, x], sibling)
-
-    def share(i):
-        at, got = pl.ds(pieces[i][1], GATHER), dests[i][1]
-        for k in (1, 3, 2):
-            j = (x + k) % NX
-            here = got.at[rows(c * NX + j, BLK), at]
-            arrived(here, x_send.at[i, 0], x_recv.at[i, j])
-            send(here, here, c_send.at[i, k], c_recv.at[i, j], sibling)
-
-    def shared(i):
-        at, got = pl.ds(pieces[i][1], GATHER), dests[i][1]
-        for k in range(NX):
-            j = (x + k) % NX
-            arrived(got.at[rows((1 - c) * NX + j, BLK), at], c_send.at[i, 0], c_recv.at[i, j])
-
-    for i in x_pieces[:1]:
-        dispatch(i, sel)
+    for i in x_pieces[1:]:
+        dispatch(i, late_sel)
+    dispatch_early(dy_pieces, early_gate)
     for i in dy_pieces:
         relay(i, 3)
-    for i in x_pieces[1:]:
-        dispatch(i, sel)
     for i in dy_pieces:
-        dispatch(i, sel_gate)
+        dispatch(i, late_gate)
+    sel[...], sel_gate[...] = selectors(chosen, 0, 0, BLK)
 
     for copy in w_copies:
         copy.wait()
@@ -286,7 +340,7 @@
     for n, i in enumerate(x_pieces):
         share(i)
         shared(i)
-        at = pl.ds(pieces[i][1], GATHER)
+        at = pl.ds(*pieces[i][1:])
         by_gate, by_up = nn(rx[:, at], wg[at, :]), nn(rx[:, at], wu[at, :])
         pre_gate[...] = by_gate if n == 0 else pre_gate[...] + by_gate
         pre_up[...] = by_up if n == 0 else pre_up[...] + by_up
@@ -298,9 +352,8 @@
     slope[...] = v_up * sig * (1.0 + v_gate * (1.0 - sig))
 
     far_rows, own_rows = rows(1 - c, HALF), rows(c, HALF)
-    back_pieces = [(0, lo, OUT_W) for lo in range(0, D, OUT_W)] + [(1, lo, DX_W) for lo in range(0, D, DX_W)]
-    n_out = D // OUT_W
-    out_back, dx_back = list(range(n_out)), list(range(n_out, len(back_pieces)))
+    back_pieces = [(0, lo, width) for lo, width in cut(OUT_CUT)] + [(1, lo, width) for lo, width in cut(DX_CUT)]
+    out_back, dx_back = list(range(len(OUT_CUT))), list(range(len(OUT_CUT), len(back_pieces)))
     buffers = (
         (far_out, near_out, back_out, got_out, pout, via_out, end_out),
         (far_dx, near_dx, back_dx, got_dx, pdx, via_dx, end_dx),
@@ -337,53 +390,45 @@
             )
         got[rows(x, BLK), at] = summed[rows(x, BLK), at]
 
-    def split(i, way):
-        lo, width = back_pieces[i][1:]
-        first_part = (width // 2 + 127) // 128 * 128
-        return pl.ds(lo, first_part) if way == 0 else pl.ds(lo + first_part, width - first_part)
-
     def combine(i, selector):
         s, lo, width = back_pieces[i]
-        got, partial, via = buffers[s][3:6]
+        got, partial, via, end = buffers[s][3:]
         at = pl.ds(lo, width)
         for k in range(1, NX):
             j = (x + k) % NX
             arrived(got.at[rows(j, BLK), at], b_send.at[i, 0], b_recv.at[i, j])
         partial[:, at] = nn(selector[...], got[:, at]).astype(BF)
-        middle = rows((z + 4) % NZ, ROWS)
-        for way, k in ((0, 3), (1, 5)):
-            to = z_owner(2 if way == 0 else 6)
-            outer = rows((z + k) % NZ, ROWS)
-            send(partial.at[outer, at], via.at[rows(way, ROWS), at], a_send.at[i, way, 0], a_recv.at[i, way, 0], to)
-            half = split(i, way)
-            send(partial.at[middle, half], via.at[rows(2 + way, ROWS), half], a_send.at[i, way, 1], a_recv.at[i, way, 1], to)
+        for n, (block, to) in enumerate((
+            (5, skip[0]),
+            (6, skip[1]),
+            (7, device(x, y, by_core((z + 2) % NZ, (z + 6) % NZ), c)),
+        )):
+            send(partial.at[rows(block, ROWS), at], via.at[rows(n, ROWS), at], a_send.at[i, n], a_recv.at[i, n], to)
+        plain = by_core((z + 6) % NZ, (z + 2) % NZ)
+        send(partial.at[rows(by_core(4, 3), ROWS), at], end.at[rows(3, ROWS), at], p_send.at[i, 3], p_recv.at[i, 3], device(x, y, plain, c))
 
     def send_home(i):
         s, lo, width = back_pieces[i]
         partial, via, end = buffers[s][4:]
         at = pl.ds(lo, width)
-        for way, k in ((0, 1), (1, 7)):
-            outer, half = rows(way, ROWS), split(i, way)
-            arrived(via.at[outer, at], a_send.at[i, way, 0], a_recv.at[i, way, 0])
-            spot = rows((z + k) % NZ, ROWS)
-            partial[spot, at] = (partial[spot, at].astype(F32) + via[outer, at].astype(F32)).astype(BF)
-            send(partial.at[spot, at], end.at[rows(way, ROWS), at], p_send.at[i, way, 0], p_recv.at[i, way, 0], z_owner(k))
-            inner = rows(2 + way, ROWS)
-            arrived(via.at[inner, half], a_send.at[i, way, 1], a_recv.at[i, way, 1])
-            spot = rows((z + 2 * k) % NZ, ROWS)
-            partial[spot, half] = (partial[spot, half].astype(F32) + via[inner, half].astype(F32)).astype(BF)
-            send(partial.at[spot, at], end.at[inner, at], p_send.at[i, way, 1], p_recv.at[i, way, 1], z_owner((2 * k) % NZ))
+        inner = by_core((z + 2) % NZ, (z + 6) % NZ)
+        for n, (block, to) in enumerate((
+            (1, z_owner(1)), (2, z_owner(7)), (by_core(3, 4), device(x, y, inner, c)),
+        )):
+            here, spot = rows(n, ROWS), rows(block, ROWS)
+            arrived(via.at[here, at], a_send.at[i, n], a_recv.at[i, n])
+            partial[spot, at] = (partial[spot, at].astype(F32) + via[here, at].astype(F32)).astype(BF)
+            send(partial.at[spot, at], end.at[here, at], p_send.at[i, n], p_recv.at[i, n], to)
 
     def finish(i, result):
         s, lo, width = back_pieces[i]
         partial, _, end = buffers[s][4:]
         at = pl.ds(lo, width)
-        total = partial[mine, at].astype(F32)
-        for n in range(2):
-            for way in range(2):
-                there = rows(2 * n + way, ROWS)
-                arrived(end.at[there, at], p_send.at[i, way, n], p_recv.at[i, way, n])
-                total = total + end[there, at].astype(F32)
+        total = partial[:ROWS, at].astype(F32)
+        for n in (3, 0, 1, 2):
+            here = rows(n, ROWS)
+            arrived(end.at[here, at], p_send.at[i, n], p_recv.at[i, n])
+            total = total + end[here, at].astype(F32)
         result[:, at] = total.astype(BF)
 
     back(out_back)
@@ -393,11 +438,12 @@
     for i in dy_pieces:
         share(i)
         shared(i)
-        at = pl.ds(pieces[i][1], GATHER)
+        at = pl.ds(*pieces[i][1:])
         back_hidden = back_hidden + nt(rdy[:, at], wd[:, at])
     gpre[:, :H] = (back_hidden * slope[...]).astype(BF)
     gpre[:, H:] = (back_hidden * act[...]).astype(BF)
     back(dx_back)
+    early = len(sent)
     for i in dx_back:
         give_back(i)
     combine(out_back[0], sel_gate)
@@ -414,6 +460,8 @@
     ]
     for copy in g_copies:
         copy.start()
+    for copy in sent[:early]:
+        copy.wait_send()
 
     todo = [(i, sel_gate) for i in out_back[1:]] + [(i, sel) for i in dx_back]
     last = out_back[0]
@@ -426,7 +474,7 @@
         finish(i, mixed)
     for i in dx_back:
         finish(i, token_grad)
-    for copy in sent:
+    for copy in sent[early:]:
         copy.wait_send()
 
     @pl.when(z_lo == 1)
@@ -463,8 +511,8 @@
     vmem = pl.BlockSpec(memory_space=pltpu.VMEM)
     hbm = pl.BlockSpec(memory_space=pl.ANY)
     dma = pltpu.SemaphoreType.DMA
-    n_gather = 1 + 2 * (D // GATHER)
-    n_back = D // OUT_W + D // DX_W
+    n_gather = 1 + len(X_CUT) + len(DY_CUT)
+    n_back = len(OUT_CUT) + len(DX_CUT)
     results = pl.pallas_call(
         kernel,
         out_shape=(
@@ -522,18 +570,18 @@
             dma((n_gather, 2, HOPS + 1)),
             dma((n_gather, 2, 2)),
             dma((n_gather, 2, 2)),
-            dma((n_gather, NX)),
-            dma((n_gather, NX)),
+            dma((n_gather + 1, NX)),
+            dma((n_gather + 1, NX)),
             dma((n_gather, NX)),
             dma((n_gather, NX)),
             dma((n_back,)),
             dma((n_back,)),
             dma((n_back, NX)),
             dma((n_back, NX)),
-            dma((n_back, 2, 2)),
-            dma((n_back, 2, 2)),
-            dma((n_back, 2, 2)),
-            dma((n_back, 2, 2)),
+            dma((n_back, 3)),
+            dma((n_back, 3)),
+            dma((n_back, 4)),
+            dma((n_back, 4)),
             dma((3,)),
         ],
         compiler_params=pltpu.CompilerParams(

time: 87.2 us -> 81.7 us (0.937)
  Pallas kernels: 86.4 us -> 80.9 us
    pallas_call x1, Pallas kernels: 83.6 us -> 78.1 us  [shards(): pl.pallas_call(kernel, out_shape=(pltpu.VMEM((ROWS, D), BF), pltpu.VMEM((...]
where the time goes in v4:
time: 81.7 us; the launch traced here: 81.5 us
  Pallas kernels  80.9 us (99%)
    pallas_call x1, Pallas kernels, shards(): pl.pallas_call(kernel, out_shape=(pltpu.VMEM((ROWS, D), BF), pltpu.VMEM((...  78.1 us
    pallas_call x1, Pallas kernels, shards(): pl.pallas_call(copy_kernel, out_shape=tuple((jax.ShapeDtypeStruct(r.shape...  2.76 us

profile of v4, /device:TPU:1, one launch (start us, length us, event | category | flops | bytes accessed | tf_op | source)
XLA Modules:
  0.0 81.5 jit_solution(13257663502494598373)
XLA Ops:
  0.6 78.1 %shard_map.128 = (bf16[16,2560]{1,0:T(8,128)(2,1)S(1)}, bf16[16,2560]{1,0:T(8,128)(2,1)S(1)}, bf16[1,2560,384]{2,1,0:T(8,128)(2,1)S(1)}, bf16[1,2560,384]{2,1,0:T(8,128)(2,1)S(1)}, bf16[1,384,2560]{2,1,0:T(8,128)(2,1)S(1)}) custom-call(bf16[16,2560]{1,0:T(8,128)(2,1)} %tokens.1, bf16[16,2560]{1,0:T(8,128)(2,1)} %grad_out.1, s32[6,16]{1,0:T(8,128)} %bitcast.2, ...), custom_call_target="tpu_custom_call" | custom-call | tf_op jit(solution)/shard_map/pallas_call | solution.py:516
  78.8 2.8 %shard_map.129 = (bf16[16,2560]{1,0:T(8,128)(2,1)}, bf16[16,2560]{1,0:T(8,128)(2,1)}, bf16[1,2560,384]{2,1,0:T(8,128)(2,1)}, bf16[1,2560,384]{2,1,0:T(8,128)(2,1)}, bf16[1,384,2560]{2,1,0:T(8,128)(2,1)}) custom-call(bf16[16,2560]{1,0:T(8,128)(2,1)S(1)} %get-tuple-element.10.refs_0_, bf16[16,2560]{1,0:T(8,128)(2,1)S(1)} %get-tuple-element.11.refs_1_, ...), custom_call_target="tpu_custom_call" | custom-call | tf_op jit(solution)/shard_map/pallas_call | solution.py:591

commit v5 on v4

--- a/solution.py
+++ b/solution.py
@@ -252,7 +252,6 @@
 
     my_slot = rows(c * NX + x, BLK)
     dests = {i: (sx, rx) for i in x_pieces} | {i: (sdy, rdy) for i in dy_pieces}
-    first_of = {x_pieces[0]: 0, dy_pieces[0]: len(pieces)}
 
     def hand_out(out, got, at, lo, count, n):
         here = pl.ds(pl.multiple_of((c * NX + x) * BLK + lo, 16), count)
@@ -269,18 +268,23 @@
         picked = tn(selector, ordered(buf, 0, 3, slice(None))).astype(BF)
         for j in range(NX):
             out[j * BLK:j * BLK + EARLY, :] = picked[j * EARLY:(j + 1) * EARLY, :]
-        hand_out(out, got, pl.ds(0, D), 0, EARLY, first_of[todo[0]])
+        hand_out(out, got, pl.ds(0, D), 0, EARLY, 0)
 
     def dispatch(i, selector):
         buf, lo, width = pieces[i]
         out, got = dests[i]
         at = pl.ds(lo, width)
         gathered(i)
-        picked = tn(selector, ordered(buf, 2, NZ, at)).astype(BF)
-        late = BLK - EARLY
-        for j in range(NX):
-            out[j * BLK + EARLY:(j + 1) * BLK, at] = picked[j * late:(j + 1) * late, :]
-        hand_out(out, got, at, EARLY, late, i)
+        if i in dy_pieces:
+            y_arrived(i, 1)
+            out[:, at] = tn(selector, ordered(buf, 0, NZ, at)).astype(BF)
+            hand_out(out, got, at, 0, BLK, i)
+        else:
+            picked = tn(selector, ordered(buf, 2, NZ, at)).astype(BF)
+            late = BLK - EARLY
+            for j in range(NX):
+                out[j * BLK + EARLY:(j + 1) * BLK, at] = picked[j * late:(j + 1) * late, :]
+            hand_out(out, got, at, EARLY, late, i)
         send(got.at[my_slot, at], got.at[my_slot, at], c_send.at[i, 0], c_recv.at[i, x], sibling)
 
     def share(i):
@@ -288,11 +292,14 @@
         for k in (1, 3, 2):
             j = (x + k) % NX
             here = got.at[rows(c * NX + j, BLK), at]
-            if i in first_of:
-                n, early_rows = first_of[i], pl.ds(pl.multiple_of((c * NX + j) * BLK, 16), EARLY)
-                arrived(got.at[early_rows], x_send.at[n, 0], x_recv.at[n, j])
-            late_rows = pl.ds(pl.multiple_of((c * NX + j) * BLK + EARLY, 16), BLK - EARLY)
-            arrived(got.at[late_rows, at], x_send.at[i, 0], x_recv.at[i, j])
+            if i == x_pieces[0]:
+                early_rows = pl.ds(pl.multiple_of((c * NX + j) * BLK, 16), EARLY)
+                arrived(got.at[early_rows], x_send.at[0, 0], x_recv.at[0, j])
+            if i in x_pieces:
+                late_rows = pl.ds(pl.multiple_of((c * NX + j) * BLK + EARLY, 16), BLK - EARLY)
+                arrived(got.at[late_rows, at], x_send.at[i, 0], x_recv.at[i, j])
+            else:
+                arrived(here, x_send.at[i, 0], x_recv.at[i, j])
             send(here, here, c_send.at[i, k], c_recv.at[i, j], sibling)
 
     def shared(i):
@@ -313,7 +320,7 @@
     for i in dy_pieces:
         start(i)
     y_arrived(0, 1)
-    early_sel, early_gate = selectors(choices(0, 3), 0, 0, EARLY)
+    early_sel = selectors(choices(0, 3), 0, 0, EARLY)[0]
     dispatch_early(x_pieces, early_sel)
     for i in [0] + x_pieces:
         relay(i, 3)
@@ -321,18 +328,17 @@
         relay(i, 1)
     gathered(0)
     chosen = choices(0, NZ)
-    late_sel, late_gate = selectors([[v[2 * ROWS:] for v in vs] for vs in chosen], 2, EARLY, BLK - EARLY)
+    late_sel = selectors([[v[2 * ROWS:] for v in vs] for vs in chosen], 2, EARLY, BLK - EARLY)[0]
     dispatch(x_pieces[0], late_sel)
     for i in dy_pieces:
         relay(i, 2)
     for i in x_pieces[1:]:
         dispatch(i, late_sel)
-    dispatch_early(dy_pieces, early_gate)
+    sel[...], sel_gate[...] = selectors(chosen, 0, 0, BLK)
     for i in dy_pieces:
         relay(i, 3)
     for i in dy_pieces:
-        dispatch(i, late_gate)
-    sel[...], sel_gate[...] = selectors(chosen, 0, 0, BLK)
+        dispatch(i, sel_gate[...])
 
     for copy in w_copies:
         copy.wait()
@@ -570,8 +576,8 @@
             dma((n_gather, 2, HOPS + 1)),
             dma((n_gather, 2, 2)),
             dma((n_gather, 2, 2)),
-            dma((n_gather + 1, NX)),
-            dma((n_gather + 1, NX)),
+            dma((n_gather, NX)),
+            dma((n_gather, NX)),
             dma((n_gather, NX)),
             dma((n_gather, NX)),
             dma((n_back,)),

time: 81.7 us -> 81.7 us (level)
  no operation moved by 1% of the time
where the time goes in v5:
time: 81.7 us; the launch traced here: 81.5 us
  Pallas kernels  80.9 us (99%)
    pallas_call x1, Pallas kernels, shards(): pl.pallas_call(kernel, out_shape=(pltpu.VMEM((ROWS, D), BF), pltpu.VMEM((...  78.1 us
    pallas_call x1, Pallas kernels, shards(): pl.pallas_call(copy_kernel, out_shape=tuple((jax.ShapeDtypeStruct(r.shape...  2.76 us

profile of v5, /device:TPU:1, one launch (start us, length us, event | category | flops | bytes accessed | tf_op | source)
XLA Modules:
  0.0 81.5 jit_solution(11145194153682502725)
XLA Ops:
  0.6 78.1 %shard_map.128 = (bf16[16,2560]{1,0:T(8,128)(2,1)S(1)}, bf16[16,2560]{1,0:T(8,128)(2,1)S(1)}, bf16[1,2560,384]{2,1,0:T(8,128)(2,1)S(1)}, bf16[1,2560,384]{2,1,0:T(8,128)(2,1)S(1)}, bf16[1,384,2560]{2,1,0:T(8,128)(2,1)S(1)}) custom-call(bf16[16,2560]{1,0:T(8,128)(2,1)} %tokens.1, bf16[16,2560]{1,0:T(8,128)(2,1)} %grad_out.1, s32[6,16]{1,0:T(8,128)} %bitcast.2, ...), custom_call_target="tpu_custom_call" | custom-call | tf_op jit(solution)/shard_map/pallas_call | solution.py:522
  78.8 2.8 %shard_map.129 = (bf16[16,2560]{1,0:T(8,128)(2,1)}, bf16[16,2560]{1,0:T(8,128)(2,1)}, bf16[1,2560,384]{2,1,0:T(8,128)(2,1)}, bf16[1,2560,384]{2,1,0:T(8,128)(2,1)}, bf16[1,384,2560]{2,1,0:T(8,128)(2,1)}) custom-call(bf16[16,2560]{1,0:T(8,128)(2,1)S(1)} %get-tuple-element.10.refs_0_, bf16[16,2560]{1,0:T(8,128)(2,1)S(1)} %get-tuple-element.11.refs_1_, ...), custom_call_target="tpu_custom_call" | custom-call | tf_op jit(solution)/shard_map/pallas_call | solution.py:597
